TPU v7x, 512 devices: a whole 4x8x8 slice. The times are simulated.
512 devices in a mesh: gx: 8 (over z), gy: 8 (over x, core), gz: 8 (over y).
Axes of the slice: x: 4, y: 8, z: 8, core: 2. Of those that a mesh axis runs over, the one named last changes fastest.
Arguments:
- turbulence: float32 [128, 1024, 1024], P('gz', 'gx', 'gy'), may hold values from -6 to 6
Outputs:
- coefficients: float32 [128, 1024, 1024], P('gz', 'gx', 'gy')
All inputs are finite; a program needn't handle non-finite values.
Results may differ from a plain program's by a relative error of at most 0.000075.
Values sent between devices are 32-bit elements; how exact they have to be, the bound alone decides.
A program may use at most 64 MiB of HBM per device.

v0:
```python
import jax
import jax.numpy as jnp
from jax import lax
from jax.sharding import PartitionSpec as P

LEVELS = 3


lift_alpha = -1.586134342059924
lift_beta = -0.052980118572961
lift_gamma = 0.882911075530934
lift_delta = 0.443506852043971
lift_zeta = 1.149604398860241
inverse_zeta = 1.0 / 1.149604398860241


def padded(cells, sides, width):
    for axis, dim in sides:
        count = lax.axis_size(axis)
        head = lax.slice_in_dim(cells, 0, width, axis=dim)
        tail = lax.slice_in_dim(cells, cells.shape[dim] - width, cells.shape[dim], axis=dim)
        cells = jnp.concatenate(
            [
                lax.ppermute(tail, axis, [(i, (i + 1) % count) for i in range(count)]),
                cells,
                lax.ppermute(head, axis, [((i + 1) % count, i) for i in range(count)]),
            ],
            axis=dim,
        )
    return cells


def spread_table(half_length, offset):
    rows = lax.broadcasted_iota(jnp.int32, (half_length, 2 * half_length), 0)
    columns = lax.broadcasted_iota(jnp.int32, (half_length, 2 * half_length), 1)
    return (columns == 2 * rows + offset).astype(jnp.float32)


def spread_last(values, offset):
    table = spread_table(values.shape[2], offset)
    return jnp.einsum("abj,jk->abk", values, table, precision=lax.Precision.HIGHEST)


def join_pairs(even_part, odd_part, direction):
    if direction == 2:
        return spread_last(even_part, 0) + spread_last(odd_part, 1)
    merged = jnp.stack([even_part, odd_part], axis=direction + 1)
    new_shape = list(even_part.shape)
    new_shape[direction] = new_shape[direction] * 2
    return merged.reshape(new_shape)


def lift_local(values, direction):
    length = values.shape[direction]
    half = length // 2

    def part(operand, lower, upper):
        return lax.slice_in_dim(operand, lower, upper, 1, direction)

    even_part = lax.slice_in_dim(values, 0, length, 2, direction)
    odd_part = lax.slice_in_dim(values, 1, length, 2, direction)
    odd_one = part(odd_part, 0, half - 1) + lift_alpha * (
        part(even_part, 0, half - 1) + part(even_part, 1, half)
    )
    even_one = part(even_part, 1, half - 1) + lift_beta * (
        part(odd_one, 0, half - 2) + part(odd_one, 1, half - 1)
    )
    odd_two = part(odd_one, 1, half - 2) + lift_gamma * (
        part(even_one, 0, half - 3) + part(even_one, 1, half - 2)
    )
    even_two = part(even_one, 1, half - 3) + lift_delta * (
        part(odd_two, 0, half - 4) + part(odd_two, 1, half - 3)
    )
    odd_final = part(odd_two, 1, half - 3)
    return join_pairs(even_two * lift_zeta, odd_final * inverse_zeta, direction)


def transform_level(current):
    widened = padded(current, (("gz", 0),), 4)
    current = lift_local(widened, 0)
    widened = padded(current, (("gx", 1),), 4)
    current = lift_local(widened, 1)
    widened = padded(current, (("gy", 2),), 4)
    return lift_local(widened, 2)


def place_inner(finer, coarse):
    full_shape = finer.shape
    zeros_like = jnp.zeros_like(coarse)
    spread = join_pairs(coarse, zeros_like, 0)
    spread = join_pairs(spread, jnp.zeros_like(spread), 1)
    spread = spread_last(spread, 0)
    depth_index = lax.broadcasted_iota(jnp.int32, full_shape, 0)
    row_index = lax.broadcasted_iota(jnp.int32, full_shape, 1)
    column_index = lax.broadcasted_iota(jnp.int32, full_shape, 2)
    chosen = depth_index % 2 + row_index % 2 + column_index % 2 == 0
    return jnp.where(chosen, spread, finer)


def local(turbulence):
    finished_levels = []
    current = turbulence
    for level_index in range(LEVELS):
        finished = transform_level(current)
        finished_levels.append(finished)
        current = lax.slice(finished, (0, 0, 0), finished.shape, (2, 2, 2))
    result = finished_levels[-1]
    for finer in reversed(finished_levels[:-1]):
        result = place_inner(finer, result)
    return result


def solution(mesh):
    in_specs = (P("gz", "gx", "gy"),)
    out_specs = P("gz", "gx", "gy")
    return jax.shard_map(local, mesh=mesh, in_specs=in_specs, out_specs=out_specs, check_vma=False)
```

profile of v0, /device:TPU:15, one launch (start us, length us, event | category | flops | bytes accessed | tf_op | source)
XLA Modules:
  0.0 102.4 jit_solution(394137170309124149)
XLA Ops:
  1.2 3.2 %collective-permute-start = (f32[4,128,128]{2,1,0:T(8,128)S(1)}, f32[4,128,128]{2,1,0:T(8,128)S(1)}, u32[]{:S(2)}, u32[]{:S(2)}) collective-permute-start(f32[4,128,128]{2,1,0:T(8,128)S(1)} %get-tuple-element.12), channel_id=1, source_target_pairs={{0,1},{1,2},{2,3},{3,4},{4,5},{5,6},{6,7},{7,0},{8,9},{9,10},{10,1... | collective-permute-start | bytes 786440 | tf_op jit(solution)/shard_map/ppermute | solution.py:24
  4.4 2.1 %collective-permute-start.1 = (f32[4,128,128]{2,1,0:T(8,128)S(1)}, f32[4,128,128]{2,1,0:T(8,128)S(1)}, u32[]{:S(2)}, u32[]{:S(2)}) collective-permute-start(f32[4,128,128]{2,1,0:T(8,128)S(1)} %get-tuple-element.11), channel_id=1, source_target_pairs={{1,0},{2,1},{3,2},{4,3},{5,4},{6,5},{7,6},{0,7},{9,8},{10,9},{11,1... | collective-permute-start | bytes 786440 | tf_op jit(solution)/shard_map/ppermute | solution.py:26
  6.5 3.7 %collective-permute-done = f32[4,128,128]{2,1,0:T(8,128)S(1)} collective-permute-done((f32[4,128,128]{2,1,0:T(8,128)S(1)}, f32[4,128,128]{2,1,0:T(8,128)S(1)}, u32[]{:S(2)}, u32[]{:S(2)}) %collective-permute-start) | collective-permute-done | bytes 262176 | tf_op jit(solution)/shard_map/ppermute | solution.py:24
  10.3 2.8 %collective-permute-done.1 = f32[4,128,128]{2,1,0:T(8,128)S(1)} collective-permute-done((f32[4,128,128]{2,1,0:T(8,128)S(1)}, f32[4,128,128]{2,1,0:T(8,128)S(1)}, u32[]{:S(2)}, u32[]{:S(2)}) %collective-permute-start.1) | collective-permute-done | bytes 262176 | tf_op jit(solution)/shard_map/ppermute | solution.py:26
  13.8 4.0 %collective-permute-start.2 = (f32[16,4,128]{2,1,0:T(4,128)S(1)}, f32[16,4,128]{2,1,0:T(4,128)S(1)}, u32[]{:S(2)}, u32[]{:S(2)}) collective-permute-start(f32[16,4,128]{2,1,0:T(4,128)S(1)} %get-tuple-element.9), channel_id=1, source_target_pairs={{0,64},{64,128},{128,192},{192,256},{256,320},{320,384},{384,448},... | collective-permute-start | bytes 98312 | tf_op jit(solution)/shard_map/ppermute | solution.py:24
  17.8 8.6 %collective-permute-start.3 = (f32[16,4,128]{2,1,0:T(4,128)S(1)}, f32[16,4,128]{2,1,0:T(4,128)S(1)}, u32[]{:S(2)}, u32[]{:S(2)}) collective-permute-start(f32[16,4,128]{2,1,0:T(4,128)S(1)} %get-tuple-element.10), channel_id=1, source_target_pairs={{64,0},{128,64},{192,128},{256,192},{320,256},{384,320},{448,384},... | collective-permute-start | bytes 98312 | tf_op jit(solution)/shard_map/ppermute | solution.py:26
  29.7 2.8 %collective-permute-start.4 = (f32[16,128,4]{1,2,0:T(4,128)S(1)}, f32[16,128,4]{1,2,0:T(4,128)S(1)}, u32[]{:S(2)}, u32[]{:S(2)}) collective-permute-start(f32[16,128,4]{1,2,0:T(4,128)S(1)} %get-tuple-element.7), channel_id=1, source_target_pairs={{0,8},{8,16},{16,24},{24,32},{32,40},{40,48},{48,56},{56,0},{1,9},... | collective-permute-start | bytes 98312 | tf_op jit(solution)/shard_map/ppermute | solution.py:24
  33.5 3.5 %collective-permute-done.5 = f32[16,128,4]{1,2,0:T(4,128)S(1)} collective-permute-done((f32[16,128,4]{1,2,0:T(4,128)S(1)}, f32[16,128,4]{1,2,0:T(4,128)S(1)}, u32[]{:S(2)}, u32[]{:S(2)}) %collective-permute-start.5) | collective-permute-done | bytes 32800 | tf_op jit(solution)/shard_map/ppermute | solution.py:26
  40.1 5.0 %slice.489 = f32[8,64,64]{2,1,0:T(8,128)S(1)} slice(f32[16,128,128]{2,1,0:T(8,128)S(1)} %convolution_add_fusion), slice={[0:16:2], [0:128:2], [0:128:2]} | slice | bytes 262144 | tf_op jit(solution)/shard_map/slice | solution.py:106
  45.1 4.3 %collective-permute-start.6 = (f32[4,64,64]{2,1,0:T(8,128)S(1)}, f32[4,64,64]{2,1,0:T(8,128)S(1)}, u32[]{:S(2)}, u32[]{:S(2)}) collective-permute-start(f32[4,64,64]{2,1,0:T(8,128)S(1)} %get-tuple-element.23), channel_id=1, source_target_pairs={{0,1},{1,2},{2,3},{3,4},{4,5},{5,6},{6,7},{7,0},{8,9},{9,10},{10,1... | collective-permute-start | bytes 196616 | tf_op jit(solution)/shard_map/ppermute | solution.py:24
  49.4 1.9 %collective-permute-start.7 = (f32[4,64,64]{2,1,0:T(8,128)S(1)}, f32[4,64,64]{2,1,0:T(8,128)S(1)}, u32[]{:S(2)}, u32[]{:S(2)}) collective-permute-start(f32[4,64,64]{2,1,0:T(8,128)S(1)} %get-tuple-element.24), channel_id=1, source_target_pairs={{1,0},{2,1},{3,2},{4,3},{5,4},{6,5},{7,6},{0,7},{9,8},{10,9},{11,1... | collective-permute-start | bytes 196616 | tf_op jit(solution)/shard_map/ppermute | solution.py:26
  51.9 5.0 %collective-permute-done.7 = f32[4,64,64]{2,1,0:T(8,128)S(1)} collective-permute-done((f32[4,64,64]{2,1,0:T(8,128)S(1)}, f32[4,64,64]{2,1,0:T(8,128)S(1)}, u32[]{:S(2)}, u32[]{:S(2)}) %collective-permute-start.7) | collective-permute-done | bytes 65568 | tf_op jit(solution)/shard_map/ppermute | solution.py:26
  57.2 1.9 %collective-permute-start.8 = (f32[8,4,64]{2,1,0:T(4,128)S(1)}, f32[8,4,64]{2,1,0:T(4,128)S(1)}, u32[]{:S(2)}, u32[]{:S(2)}) collective-permute-start(f32[8,4,64]{2,1,0:T(4,128)S(1)} %get-tuple-element.21), channel_id=1, source_target_pairs={{0,64},{64,128},{128,192},{192,256},{256,320},{320,384},{384,448},... | collective-permute-start | bytes 24584 | tf_op jit(solution)/shard_map/ppermute | solution.py:24
  59.2 5.2 %collective-permute-start.9 = (f32[8,4,64]{2,1,0:T(4,128)S(1)}, f32[8,4,64]{2,1,0:T(4,128)S(1)}, u32[]{:S(2)}, u32[]{:S(2)}) collective-permute-start(f32[8,4,64]{2,1,0:T(4,128)S(1)} %get-tuple-element.22), channel_id=1, source_target_pairs={{64,0},{128,64},{192,128},{256,192},{320,256},{384,320},{448,384},... | collective-permute-start | bytes 24584 | tf_op jit(solution)/shard_map/ppermute | solution.py:26
  66.0 2.3 %collective-permute-start.10 = (f32[8,64,4]{1,2,0:T(4,128)S(1)}, f32[8,64,4]{1,2,0:T(4,128)S(1)}, u32[]{:S(2)}, u32[]{:S(2)}) collective-permute-start(f32[8,64,4]{1,2,0:T(4,128)S(1)} %get-tuple-element.19), channel_id=1, source_target_pairs={{0,8},{8,16},{16,24},{24,32},{32,40},{40,48},{48,56},{56,0},{1,9},... | collective-permute-start | bytes 24584 | tf_op jit(solution)/shard_map/ppermute | solution.py:24
  69.2 3.5 %collective-permute-done.11 = f32[8,64,4]{1,2,0:T(4,128)S(1)} collective-permute-done((f32[8,64,4]{1,2,0:T(4,128)S(1)}, f32[8,64,4]{1,2,0:T(4,128)S(1)}, u32[]{:S(2)}, u32[]{:S(2)}) %collective-permute-start.11) | collective-permute-done | bytes 8224 | tf_op jit(solution)/shard_map/ppermute | solution.py:26
  74.8 3.4 %collective-permute-start.12 = (f32[4,32,32]{2,1,0:T(8,128)S(1)}, f32[4,32,32]{2,1,0:T(8,128)S(1)}, u32[]{:S(2)}, u32[]{:S(2)}) collective-permute-start(f32[4,32,32]{2,1,0:T(8,128)S(1)} %slice.538), channel_id=1, source_target_pairs={{0,1},{1,2},{2,3},{3,4},{4,5},{5,6},{6,7},{7,0},{8,9},{9,10},{10,1... | collective-permute-start | bytes 49160 | tf_op jit(solution)/shard_map/ppermute | solution.py:24
  78.2 1.9 %collective-permute-start.13 = (f32[4,32,32]{2,1,0:T(8,128)S(1)}, f32[4,32,32]{2,1,0:T(8,128)S(1)}, u32[]{:S(2)}, u32[]{:S(2)}) collective-permute-start(f32[4,32,32]{2,1,0:T(8,128)S(1)} %slice.538), channel_id=1, source_target_pairs={{1,0},{2,1},{3,2},{4,3},{5,4},{6,5},{7,6},{0,7},{9,8},{10,9},{11,1... | collective-permute-start | bytes 49160 | tf_op jit(solution)/shard_map/ppermute | solution.py:26
  80.2 3.1 %collective-permute-done.13 = f32[4,32,32]{2,1,0:T(8,128)S(1)} collective-permute-done((f32[4,32,32]{2,1,0:T(8,128)S(1)}, f32[4,32,32]{2,1,0:T(8,128)S(1)}, u32[]{:S(2)}, u32[]{:S(2)}) %collective-permute-start.13) | collective-permute-done | bytes 16416 | tf_op jit(solution)/shard_map/ppermute | solution.py:26
  83.4 3.5 %collective-permute-start.14 = (f32[4,4,32]{2,1,0:T(4,128)S(1)}, f32[4,4,32]{2,1,0:T(4,128)S(1)}, u32[]{:S(2)}, u32[]{:S(2)}) collective-permute-start(f32[4,4,32]{2,1,0:T(4,128)S(1)} %get-tuple-element.33), channel_id=1, source_target_pairs={{0,64},{64,128},{128,192},{192,256},{256,320},{320,384},{384,448},... | collective-permute-start | bytes 6152 | tf_op jit(solution)/shard_map/ppermute | solution.py:24
  86.9 3.5 %collective-permute-start.15 = (f32[4,4,32]{2,1,0:T(4,128)S(1)}, f32[4,4,32]{2,1,0:T(4,128)S(1)}, u32[]{:S(2)}, u32[]{:S(2)}) collective-permute-start(f32[4,4,32]{2,1,0:T(4,128)S(1)} %get-tuple-element.34), channel_id=1, source_target_pairs={{64,0},{128,64},{192,128},{256,192},{320,256},{384,320},{448,384},... | collective-permute-start | bytes 6152 | tf_op jit(solution)/shard_map/ppermute | solution.py:26
  92.0 2.5 %collective-permute-start.16 = (f32[4,32,4]{1,2,0:T(4,128)S(1)}, f32[4,32,4]{1,2,0:T(4,128)S(1)}, u32[]{:S(2)}, u32[]{:S(2)}) collective-permute-start(f32[4,32,4]{1,2,0:T(4,128)S(1)} %get-tuple-element.31), channel_id=1, source_target_pairs={{0,8},{8,16},{16,24},{24,32},{32,40},{40,48},{48,56},{56,0},{1,9},... | collective-permute-start | bytes 6152 | tf_op jit(solution)/shard_map/ppermute | solution.py:24
  95.4 3.5 %collective-permute-done.17 = f32[4,32,4]{1,2,0:T(4,128)S(1)} collective-permute-done((f32[4,32,4]{1,2,0:T(4,128)S(1)}, f32[4,32,4]{1,2,0:T(4,128)S(1)}, u32[]{:S(2)}, u32[]{:S(2)}) %collective-permute-start.17) | collective-permute-done | bytes 2080 | tf_op jit(solution)/shard_map/ppermute | solution.py:26
  100.5 1.9 %convolution_select_fusion = f32[16,128,128]{2,1,0:T(8,128)} fusion(f32[16,128,128]{2,1,0:T(8,128)S(1)} %convolution_add_fusion, f32[16,128,64]{2,0,1:T(8,128)S(1)} %bitcast.66, s32[128]{0:T(128)S(1)} %get-tuple-element.43, s32[128]{0:T(128)S(1)} %get-tuple-element.44, s32[16]{0:T(128)S(1)} %get-tuple-element.45, s32[16]{0:T(128)S(1)} %get-tuple-element.46, ...), kind=kOutput, calls=%fused_computation | convolution fusion | flops 203169792 | bytes 2622992 | tf_op jit(solution)/shard_map/abj,jk->abk/dot_general | solution.py:41
  (125 shorter events, 18.4 us)
Async XLA Ops:
  0.0 10.3 %copy-start = (f32[16,128,128]{2,1,0:T(8,128)S(1)}, f32[16,128,128]{2,1,0:T(8,128)}, u32[]{:S(2)}) copy-start(f32[16,128,128]{2,1,0:T(8,128)} %param.1) | copy-start | bytes 3145732
  1.2 9.1 %collective-permute-start = (f32[4,128,128]{2,1,0:T(8,128)S(1)}, f32[4,128,128]{2,1,0:T(8,128)S(1)}, u32[]{:S(2)}, u32[]{:S(2)}) collective-permute-start(f32[4,128,128]{2,1,0:T(8,128)S(1)} %get-tuple-element.12), channel_id=1, source_target_pairs={{0,1},{1,2},{2,3},{3,4},{4,5},{5,6},{6,7},{7,0},{8,9},{9,10},{10,1... | collective-permute-start | bytes 786440 | tf_op jit(solution)/shard_map/ppermute | solution.py:24
  4.4 8.8 %collective-permute-start.1 = (f32[4,128,128]{2,1,0:T(8,128)S(1)}, f32[4,128,128]{2,1,0:T(8,128)S(1)}, u32[]{:S(2)}, u32[]{:S(2)}) collective-permute-start(f32[4,128,128]{2,1,0:T(8,128)S(1)} %get-tuple-element.11), channel_id=1, source_target_pairs={{1,0},{2,1},{3,2},{4,3},{5,4},{6,5},{7,6},{0,7},{9,8},{10,9},{11,1... | collective-permute-start | bytes 786440 | tf_op jit(solution)/shard_map/ppermute | solution.py:26
  13.8 12.6 %collective-permute-start.2 = (f32[16,4,128]{2,1,0:T(4,128)S(1)}, f32[16,4,128]{2,1,0:T(4,128)S(1)}, u32[]{:S(2)}, u32[]{:S(2)}) collective-permute-start(f32[16,4,128]{2,1,0:T(4,128)S(1)} %get-tuple-element.9), channel_id=1, source_target_pairs={{0,64},{64,128},{128,192},{192,256},{256,320},{320,384},{384,448},... | collective-permute-start | bytes 98312 | tf_op jit(solution)/shard_map/ppermute | solution.py:24
  17.8 9.6 %collective-permute-start.3 = (f32[16,4,128]{2,1,0:T(4,128)S(1)}, f32[16,4,128]{2,1,0:T(4,128)S(1)}, u32[]{:S(2)}, u32[]{:S(2)}) collective-permute-start(f32[16,4,128]{2,1,0:T(4,128)S(1)} %get-tuple-element.10), channel_id=1, source_target_pairs={{64,0},{128,64},{192,128},{256,192},{320,256},{384,320},{448,384},... | collective-permute-start | bytes 98312 | tf_op jit(solution)/shard_map/ppermute | solution.py:26
  29.7 3.8 %collective-permute-start.4 = (f32[16,128,4]{1,2,0:T(4,128)S(1)}, f32[16,128,4]{1,2,0:T(4,128)S(1)}, u32[]{:S(2)}, u32[]{:S(2)}) collective-permute-start(f32[16,128,4]{1,2,0:T(4,128)S(1)} %get-tuple-element.7), channel_id=1, source_target_pairs={{0,8},{8,16},{16,24},{24,32},{32,40},{40,48},{48,56},{56,0},{1,9},... | collective-permute-start | bytes 98312 | tf_op jit(solution)/shard_map/ppermute | solution.py:24
  32.5 4.6 %collective-permute-start.5 = (f32[16,128,4]{1,2,0:T(4,128)S(1)}, f32[16,128,4]{1,2,0:T(4,128)S(1)}, u32[]{:S(2)}, u32[]{:S(2)}) collective-permute-start(f32[16,128,4]{1,2,0:T(4,128)S(1)} %get-tuple-element.8), channel_id=1, source_target_pairs={{8,0},{16,8},{24,16},{32,24},{40,32},{48,40},{56,48},{0,56},{9,1},... | collective-permute-start | bytes 98312 | tf_op jit(solution)/shard_map/ppermute | solution.py:26
  45.1 6.7 %collective-permute-start.6 = (f32[4,64,64]{2,1,0:T(8,128)S(1)}, f32[4,64,64]{2,1,0:T(8,128)S(1)}, u32[]{:S(2)}, u32[]{:S(2)}) collective-permute-start(f32[4,64,64]{2,1,0:T(8,128)S(1)} %get-tuple-element.23), channel_id=1, source_target_pairs={{0,1},{1,2},{2,3},{3,4},{4,5},{5,6},{6,7},{7,0},{8,9},{9,10},{10,1... | collective-permute-start | bytes 196616 | tf_op jit(solution)/shard_map/ppermute | solution.py:24
  49.4 7.5 %collective-permute-start.7 = (f32[4,64,64]{2,1,0:T(8,128)S(1)}, f32[4,64,64]{2,1,0:T(8,128)S(1)}, u32[]{:S(2)}, u32[]{:S(2)}) collective-permute-start(f32[4,64,64]{2,1,0:T(8,128)S(1)} %get-tuple-element.24), channel_id=1, source_target_pairs={{1,0},{2,1},{3,2},{4,3},{5,4},{6,5},{7,6},{0,7},{9,8},{10,9},{11,1... | collective-permute-start | bytes 196616 | tf_op jit(solution)/shard_map/ppermute | solution.py:26
  57.2 7.1 %collective-permute-start.8 = (f32[8,4,64]{2,1,0:T(4,128)S(1)}, f32[8,4,64]{2,1,0:T(4,128)S(1)}, u32[]{:S(2)}, u32[]{:S(2)}) collective-permute-start(f32[8,4,64]{2,1,0:T(4,128)S(1)} %get-tuple-element.21), channel_id=1, source_target_pairs={{0,64},{64,128},{128,192},{192,256},{256,320},{320,384},{384,448},... | collective-permute-start | bytes 24584 | tf_op jit(solution)/shard_map/ppermute | solution.py:24
  59.2 6.0 %collective-permute-start.9 = (f32[8,4,64]{2,1,0:T(4,128)S(1)}, f32[8,4,64]{2,1,0:T(4,128)S(1)}, u32[]{:S(2)}, u32[]{:S(2)}) collective-permute-start(f32[8,4,64]{2,1,0:T(4,128)S(1)} %get-tuple-element.22), channel_id=1, source_target_pairs={{64,0},{128,64},{192,128},{256,192},{320,256},{384,320},{448,384},... | collective-permute-start | bytes 24584 | tf_op jit(solution)/shard_map/ppermute | solution.py:26
  66.0 3.1 %collective-permute-start.10 = (f32[8,64,4]{1,2,0:T(4,128)S(1)}, f32[8,64,4]{1,2,0:T(4,128)S(1)}, u32[]{:S(2)}, u32[]{:S(2)}) collective-permute-start(f32[8,64,4]{1,2,0:T(4,128)S(1)} %get-tuple-element.19), channel_id=1, source_target_pairs={{0,8},{8,16},{16,24},{24,32},{32,40},{40,48},{48,56},{56,0},{1,9},... | collective-permute-start | bytes 24584 | tf_op jit(solution)/shard_map/ppermute | solution.py:24
  68.3 4.4 %collective-permute-start.11 = (f32[8,64,4]{1,2,0:T(4,128)S(1)}, f32[8,64,4]{1,2,0:T(4,128)S(1)}, u32[]{:S(2)}, u32[]{:S(2)}) collective-permute-start(f32[8,64,4]{1,2,0:T(4,128)S(1)} %get-tuple-element.20), channel_id=1, source_target_pairs={{8,0},{16,8},{24,16},{32,24},{40,32},{48,40},{56,48},{0,56},{9,1},... | collective-permute-start | bytes 24584 | tf_op jit(solution)/shard_map/ppermute | solution.py:26
  74.8 5.3 %collective-permute-start.12 = (f32[4,32,32]{2,1,0:T(8,128)S(1)}, f32[4,32,32]{2,1,0:T(8,128)S(1)}, u32[]{:S(2)}, u32[]{:S(2)}) collective-permute-start(f32[4,32,32]{2,1,0:T(8,128)S(1)} %slice.538), channel_id=1, source_target_pairs={{0,1},{1,2},{2,3},{3,4},{4,5},{5,6},{6,7},{7,0},{8,9},{9,10},{10,1... | collective-permute-start | bytes 49160 | tf_op jit(solution)/shard_map/ppermute | solution.py:24
  78.2 5.0 %collective-permute-start.13 = (f32[4,32,32]{2,1,0:T(8,128)S(1)}, f32[4,32,32]{2,1,0:T(8,128)S(1)}, u32[]{:S(2)}, u32[]{:S(2)}) collective-permute-start(f32[4,32,32]{2,1,0:T(8,128)S(1)} %slice.538), channel_id=1, source_target_pairs={{1,0},{2,1},{3,2},{4,3},{5,4},{6,5},{7,6},{0,7},{9,8},{10,9},{11,1... | collective-permute-start | bytes 49160 | tf_op jit(solution)/shard_map/ppermute | solution.py:26
  83.4 7.1 %collective-permute-start.14 = (f32[4,4,32]{2,1,0:T(4,128)S(1)}, f32[4,4,32]{2,1,0:T(4,128)S(1)}, u32[]{:S(2)}, u32[]{:S(2)}) collective-permute-start(f32[4,4,32]{2,1,0:T(4,128)S(1)} %get-tuple-element.33), channel_id=1, source_target_pairs={{0,64},{64,128},{128,192},{192,256},{256,320},{320,384},{384,448},... | collective-permute-start | bytes 6152 | tf_op jit(solution)/shard_map/ppermute | solution.py:24
  86.9 4.8 %collective-permute-start.15 = (f32[4,4,32]{2,1,0:T(4,128)S(1)}, f32[4,4,32]{2,1,0:T(4,128)S(1)}, u32[]{:S(2)}, u32[]{:S(2)}) collective-permute-start(f32[4,4,32]{2,1,0:T(4,128)S(1)} %get-tuple-element.34), channel_id=1, source_target_pairs={{64,0},{128,64},{192,128},{256,192},{320,256},{384,320},{448,384},... | collective-permute-start | bytes 6152 | tf_op jit(solution)/shard_map/ppermute | solution.py:26
  92.0 3.3 %collective-permute-start.16 = (f32[4,32,4]{1,2,0:T(4,128)S(1)}, f32[4,32,4]{1,2,0:T(4,128)S(1)}, u32[]{:S(2)}, u32[]{:S(2)}) collective-permute-start(f32[4,32,4]{1,2,0:T(4,128)S(1)} %get-tuple-element.31), channel_id=1, source_target_pairs={{0,8},{8,16},{16,24},{24,32},{32,40},{40,48},{48,56},{56,0},{1,9},... | collective-permute-start | bytes 6152 | tf_op jit(solution)/shard_map/ppermute | solution.py:24
  94.6 4.3 %collective-permute-start.17 = (f32[4,32,4]{1,2,0:T(4,128)S(1)}, f32[4,32,4]{1,2,0:T(4,128)S(1)}, u32[]{:S(2)}, u32[]{:S(2)}) collective-permute-start(f32[4,32,4]{1,2,0:T(4,128)S(1)} %get-tuple-element.32), channel_id=1, source_target_pairs={{8,0},{16,8},{24,16},{32,24},{40,32},{48,40},{56,48},{0,56},{9,1},... | collective-permute-start | bytes 6152 | tf_op jit(solution)/shard_map/ppermute | solution.py:26
where the time goes:
time: 103 us; the launch traced here: 102 us
  starting transfers between devices  51.1 us (50%)
  waiting for transfers between devices  31.3 us (30%)
  local copies, waits for them, and re-layouts  10.9 us (11%)
  matrix products  5.67 us (6%)
  other arithmetic  2.51 us (2%)
    ppermute x9, starting transfers between devices, padded(): lax.ppermute(tail, axis, [(i, (i + 1) % count) for i in range(count)])  27.9 us
    ppermute x9, waiting for transfers between devices, padded(): lax.ppermute(head, axis, [((i + 1) % count, i) for i in range(count)])  24.4 us
    ppermute x9, starting transfers between devices, padded(): lax.ppermute(head, axis, [((i + 1) % count, i) for i in range(count)])  23.2 us
    ppermute x9, waiting for transfers between devices, padded(): lax.ppermute(tail, axis, [(i, (i + 1) % count) for i in range(count)])  6.9 us
    slice x2, local copies, waits for them, and re-layouts, local(): current = lax.slice(finished, (0, 0, 0), finished.shape, (2, 2, 2))  5.85 us
    dot_general x8, matrix products, spread_last(): jnp.einsum('abj,jk->abk', values, table, precision=lax.Precision.HIGHEST)  5.67 us
  transfers between devices with their start and end apart: 18, of which 14 were waited for; matrix products, arithmetic and copies ran while one was open for 0% of the time, Pallas kernels for 0%

commit v1 on v0

v1 whole, which is shorter than its diff:
```python
import functools
import itertools

import jax
import jax.numpy as jnp
import ml_dtypes
import numpy as np
from jax import lax
from jax.experimental import pallas as pl
from jax.experimental.pallas import tpu as pltpu
from jax.sharding import PartitionSpec as P

ALPHA = -1.586134342059924
BETA = -0.052980118572961
GAMMA = 0.882911075530934
DELTA = 0.443506852043971
ZETA = 1.149604398860241
AXES = ("gz", "gx", "gy")
BF16 = ml_dtypes.bfloat16


def lifting_matrix(n):
    v = np.eye(n)
    s, d = v[0::2].copy(), v[1::2].copy()
    d = d + ALPHA * (s + np.roll(s, -1, 0))
    s = s + BETA * (np.roll(d, 1, 0) + d)
    d = d + GAMMA * (s + np.roll(s, -1, 0))
    s = s + DELTA * (np.roll(d, 1, 0) + d)
    out = np.zeros((n, n))
    out[0::2], out[1::2] = s * ZETA, d / ZETA
    return out


def blocks(n, total):
    m, k, out = np.eye(total), total, []
    p = total // n // 2
    for level in range(3):
        t = lifting_matrix(k) @ m
        rows = t[p * k * n // total : (p + 1) * k * n // total]
        out.append([rows[:, (p + o) * n : (p + o + 1) * n] for o in (-1, 0, 1)])
        m, k = t[0::2], k // 2
    return out


def split(m):
    hi = m.astype(np.float32).astype(BF16)
    lo = (m - hi.astype(np.float64)).astype(np.float32).astype(BF16)
    return hi, lo


def low_rank(m, rank):
    u, s, v = np.linalg.svd(m, full_matrices=False)
    return u[:, :rank] * s[:rank], v[:rank]


def tables(n, total):
    per_level = blocks(n, total)
    place = np.zeros((2 * n, n + n // 2 + n // 4))
    place[np.arange(n), np.arange(n)] = 1
    place[n + 2 * np.arange(n // 2), n + np.arange(n // 2)] = 1
    place[n + 4 * np.arange(n // 4) + 1, n + n // 2 + np.arange(n // 4)] = 1
    before, own, after = (place @ np.concatenate([lv[o] for lv in per_level]) for o in range(3))
    r_before, s_before = low_rank(before, 6)
    r_after, s_after = low_rank(after, 6)
    send = np.zeros((16, n))
    send[0:6], send[8:14] = s_before, s_after
    take = np.zeros((16, 2 * n))
    take[0:6], take[8:14] = r_before.T, r_after.T
    w_hi, w_lo = split(own.T)
    t_hi, t_lo = split(take)
    ext = [np.concatenate([lv[1], lv[0][:8], lv[2][-8:]]) for lv in per_level]
    g1_hi, g1_lo = split(ext[0])
    g2_hi, g2_lo = split(np.concatenate(ext[1:]))
    return dict(
        wa=np.concatenate([w_hi, w_hi]),
        wb=w_lo,
        sa=np.concatenate(split(send)),
        ra=np.concatenate([t_hi, t_hi, t_lo]),
        g1a=np.concatenate([g1_hi, g1_hi], axis=1),
        g1b=g1_lo,
        g2a=np.concatenate([g2_hi, g2_hi], axis=1),
        g2b=g2_lo,
    )


def add(*terms):
    total = None
    for coefficient, v in terms:
        if v is None:
            continue
        v = v if coefficient == 1 else v * coefficient
        total = v if total is None else total + v
    return total


def plus(base, coefficient, one, two):
    pair = one if two is None else two if one is None else one + two
    return add((1, base), (coefficient, pair))


def lift_zero_extended(v, lowest, highest, low_only=False):
    a, b = lowest // 2 - 2, highest // 2 + 3
    s = {i: v.get(2 * i) for i in range(a, b + 1)}
    d = {i: v.get(2 * i + 1) for i in range(a, b + 1)}
    d1 = {i: plus(d[i], ALPHA, s[i], s[i + 1]) for i in range(a, b)}
    s1 = {i: plus(s[i], BETA, d1[i - 1], d1[i]) for i in range(a + 1, b)}
    d2 = {i: plus(d1[i], GAMMA, s1[i], s1[i + 1]) for i in range(a + 1, b - 1)}
    s2 = {i: plus(s1[i], DELTA, d2[i - 1], d2[i]) for i in range(a + 2, b - 1)}
    out = {}
    for i in range(a + 2, b - 1):
        for k, part, scale in ((2 * i, s2[i], ZETA), (2 * i + 1, d2[i], 1 / ZETA)):
            if lowest <= k <= highest and part is not None and not (low_only and k % 2):
                out[k] = part * scale
    return out, d1, s1


def halo_parts(v):
    bf = jnp.bfloat16
    hi = v.astype(bf)
    return hi, (v - hi.astype(jnp.float32)).astype(bf)


def dot(a, b, dims=((1,), (0,))):
    return lax.dot_general(a, b, (dims, ((), ())), preferred_element_type=jnp.float32)


def neighbour(offsets):
    return {
        axis: lax.rem(lax.axis_index(axis) + (o + lax.axis_size(axis)), lax.axis_size(axis))
        for axis, o in zip(AXES, offsets)
        if o
    }


SIDES = (1, -1)
TARGETS = (
    [(0, 0, c) for c in SIDES]
    + [(0, b, 0) for b in SIDES]
    + [(a, b, 0) for a in SIDES for b in (0, 1, -1)]
    + [(2 * a, b, 0) for a in SIDES for b in (0, 1, -1)]
)


def kernel(
    x, wa, wb, sa, ra, g1a, g1b, g2a, g2b, out,
    yc, q1, q2, q3, f2, f3,
    ys, yr, xs, xr, zs, zr, ps, pr, es, er, ds, dr, cs, cr,
    send_sem, recv_sem,
):
    barrier = pltpu.get_barrier_semaphore()
    for offsets in TARGETS:
        pl.semaphore_signal(barrier, inc=1, device_id=neighbour(offsets), device_id_type=pl.DeviceIdType.MESH)

    copies = []

    def send(source, target, offsets):
        k = len(copies)
        copy = pltpu.make_async_remote_copy(
            source, target, send_sem.at[k], recv_sem.at[k],
            device_id=neighbour(offsets), device_id_type=pl.DeviceIdType.MESH,
        )
        copies.append(copy)
        copy.start()
        return copy

    nz, nx, ny = x.shape

    v = x[...].reshape(nz * nx, ny)
    hi, lo = halo_parts(v)
    first = dot(sa[...], hi, ((1,), (1,)))
    second = dot(sa[0:16], lo, ((1,), (1,)))
    message = first[0:16] + first[16:32] + second
    ys[0] = message[0:8]
    ys[1] = message[8:16]
    pl.semaphore_wait(barrier, len(TARGETS))
    y_copies = [send(ys.at[k], yr.at[k], (0, 0, c)) for k, c in enumerate(SIDES)]

    for z in range(nz):
        hi, lo = halo_parts(x[z])
        yc[z] = dot(jnp.concatenate([hi, lo], axis=1), wa[...]) + dot(hi, wb[...])

    for copy in y_copies:
        copy.wait_recv()

    for z in range(nz):
        lanes = slice(z * nx, (z + 1) * nx)
        h_hi, h_lo = halo_parts(jnp.concatenate([yr[0, :, lanes], yr[1, :, lanes]], axis=0))
        y = yc[z] + dot(jnp.concatenate([h_hi, h_lo, h_hi], axis=0), ra[...], ((0,), (0,)))
        hi, lo = halo_parts(y)
        both = jnp.concatenate([hi, lo], axis=0)
        q1[z] = dot(g1a[...], both[:, 0:128]) + dot(g1b[...], hi[:, 0:128])
        q = dot(g2a[...], both[:, 128:256]) + dot(g2b[...], hi[:, 128:256])
        q2[z] = q[0:80]
        q3[z] = q[80:128]

    for tile in range(18):
        rows = slice(8 * tile, 8 * tile + 8)
        o, d1, s1 = lift_zero_extended({k: q1[k, rows] for k in range(nz)}, 0, nz - 1)
        s_first = q1[0, rows]
        to_next = (d1[nz // 2 - 1], s1[nz // 2 - 1])
        to_previous = (s_first, s_first + BETA * d1[0])
        for k in range(nz):
            if tile < 16:
                out[k, rows] = o[k]
            else:
                xs[tile - 16, k] = o[k]
        for a, pair in enumerate((to_next, to_previous)):
            for r in range(2):
                if tile < 16:
                    zs[a, r, rows] = pair[r]
                else:
                    es[2 * a + tile - 16, r] = pair[r]
    copies_late = [send(zs.at[a], zr.at[a], (s, 0, 0)) for a, s in enumerate(SIDES)]

    lane = lax.broadcasted_iota(jnp.int32, (8, 128), 1)

    def pack2(one, two):
        two = jnp.zeros_like(one) if two is None else pltpu.roll(two, 1, 1)
        return jnp.where(lane % 2 == 0, one, two)

    def pack4(parts):
        total = parts[0]
        for k, part in enumerate(parts[1:], 1):
            total = jnp.where(lane % 4 == (1 + k) % 4, pltpu.roll(part, k, 1), total)
        return total

    for tile in range(10):
        rows = slice(8 * tile, 8 * tile + 8)
        c2, _, _ = lift_zero_extended({k: q2[k, rows] for k in range(nz)}, -4, nz + 3, True)
        c2 = {k // 2: w for k, w in c2.items()}
        o, _, _ = lift_zero_extended(c2, -6, 12)
        for k in range(8):
            if tile < 8:
                f2[k, rows] = o[k]
            else:
                xs[tile - 8, 16 + k] = o[k]
        for a, pairs in enumerate((((8, 9), (10, 11), (12, None)), ((-6, -5), (-4, -3), (-2, -1)))):
            for r, (one, two) in enumerate(pairs):
                packed = pack2(o[one], None if two is None else o[two])
                if tile < 8:
                    ps[a, 64 * r + 8 * tile : 64 * r + 8 * tile + 8] = packed
                else:
                    es[2 * a + tile - 8, 2 + r] = packed

    for tile in range(6):
        rows = slice(8 * tile, 8 * tile + 8)
        c2, _, _ = lift_zero_extended({k: q3[k, rows] for k in range(nz)}, -4, nz + 3, True)
        c2 = {k // 2: w for k, w in c2.items()}
        c3, _, _ = lift_zero_extended(c2, -6, 12, True)
        c3 = {k // 2: w for k, w in c3.items()}
        o, _, _ = lift_zero_extended(c3, -6, 10)
        zero = jnp.zeros((8, 128), jnp.float32)
        for k in range(4):
            if tile < 4:
                f3[k, rows] = o[k]
            else:
                xs[tile - 4, 24 + k] = o[k]
        near = (pack4([o[4], o[5], o[6], o[7]]), pack4([o[-4], o[-3], o[-2], o[-1]]))
        far = (pack4([o[8], o[9], o[10], zero]), pack4([zero, zero, o[-6], o[-5]]))
        for a in range(2):
            if tile < 4:
                ps[a, 192 + 8 * tile : 200 + 8 * tile] = near[a]
                ds[a, rows] = far[a]
            else:
                es[2 * a + tile - 4, 5] = near[a]
                cs[2 * a + tile - 4] = far[a]

    for b, t in enumerate(SIDES):
        copies_late.append(send(xs.at[b], xr.at[b], (0, t, 0)))
    for a, s in enumerate(SIDES):
        copies_late.append(send(ps.at[a], pr.at[a], (s, 0, 0)))
        copies_late.append(send(ds.at[a], dr.at[a], (2 * s, 0, 0)))
        for b, t in enumerate(SIDES):
            copies_late.append(send(es.at[2 * a + b], er.at[2 * a + b], (s, t, 0)))
            copies_late.append(send(cs.at[2 * a + b], cr.at[2 * a + b], (2 * s, t, 0)))
    for copy in copies_late:
        copy.wait_recv()

    for a in range(2):
        for b, (r1, r2, r3) in enumerate(((0, 0, 0), (nx - 8, nx // 2 - 8, nx // 4 - 8))):
            e = 2 * a + b
            for r in range(2):
                zr[a, r, r1 : r1 + 8] += er[e, r]
            for r in range(3):
                pr[a, 64 * r + r2 : 64 * r + r2 + 8] += er[e, 2 + r]
            pr[a, 192 + r3 : 200 + r3] += er[e, 5]
            dr[a, r3 : r3 + 8] += cr[e]

    for b, (r1, r2, r3) in enumerate(((0, 0, 0), (nx - 8, nx // 2 - 8, nx // 4 - 8))):
        for k in range(16):
            out[k, r1 : r1 + 8] += xr[b, k]
        for k in range(8):
            f2[k, r2 : r2 + 8] += xr[b, 16 + k]
        for k in range(4):
            f3[k, r3 : r3 + 8] += xr[b, 24 + k]

    for tile in range(16):
        rows = slice(8 * tile, 8 * tile + 8)
        one, two = zr[0, 0, rows], zr[0, 1, rows]
        s10 = BETA * one
        d2m = one + GAMMA * (two + s10)
        d20 = GAMMA * s10
        s20 = s10 + DELTA * (d2m + d20)
        out[0, rows] += ZETA * s20
        out[1, rows] += (1 / ZETA) * d20
        out[2, rows] += (ZETA * DELTA) * d20
        one, two = zr[1, 0, rows], zr[1, 1, rows]
        d17 = ALPHA * one
        s17 = BETA * d17
        d27 = d17 + GAMMA * (s17 + two + s17)
        d26 = GAMMA * s17
        s27 = s17 + DELTA * (d26 + d27)
        out[12, rows] += (ZETA * DELTA) * d26
        out[13, rows] += (1 / ZETA) * d26
        out[14, rows] += ZETA * s27
        out[15, rows] += (1 / ZETA) * d27

    lane3 = lax.broadcasted_iota(jnp.int32, (32, 128), 1)
    lane2 = lax.broadcasted_iota(jnp.int32, (64, 128), 1)
    for k in range(8):
        total = f2[k]
        r, second = divmod(k, 2)
        if k < 5:
            part = pr[0, 64 * r : 64 * r + 64]
            total = total + (pltpu.roll(part, 127, 1) if second else part)
        if k >= 2:
            r, second = divmod(k - 2, 2)
            part = pr[1, 64 * r : 64 * r + 64]
            total = total + (pltpu.roll(part, 127, 1) if second else part)
        f2[k] = total
        if k % 2 == 0:
            j = k // 2
            packed = pr[0, 192:224] + pr[1, 192:224] + dr[0] + dr[1]
            deep = pltpu.roll(f3[j] + pltpu.roll(packed, (128 - j) % 128, 1), 127, 1)
            even = pl.ds(0, 32, 2)
            f2[k, even, :] = jnp.where(lane3 % 4 == 0, deep, f2[k, even, :])
        even = pl.ds(0, 64, 2)
        out[2 * k, even, :] = jnp.where(lane2 % 2 == 0, f2[k], out[2 * k, even, :])

    for copy in copies:
        copy.wait_send()


def local(turbulence, consts):
    nz, nx, ny = turbulence.shape
    f32 = jnp.float32
    vmem = lambda *shape: pltpu.VMEM(shape, f32)
    pair = lambda *shape: [vmem(*shape), vmem(*shape)]
    count = 18
    return pl.pallas_call(
        kernel,
        out_shape=jax.ShapeDtypeStruct(turbulence.shape, f32),
        in_specs=[pl.BlockSpec(memory_space=pltpu.VMEM)] * (1 + len(consts)),
        out_specs=pl.BlockSpec(memory_space=pltpu.VMEM),
        scratch_shapes=[
            vmem(nz, nx, 2 * ny), vmem(nz, 144, ny), vmem(nz, 80, ny), vmem(nz, 48, ny),
            vmem(8, 64, ny), vmem(4, 32, ny),
            *pair(2, 8, nz * nx),
            *pair(2, 28, 8, ny),
            *pair(2, 2, nx, ny),
            *pair(2, 224, ny),
            *pair(4, 6, 8, ny),
            *pair(2, 32, ny),
            *pair(4, 8, ny),
            pltpu.SemaphoreType.DMA((count,)),
            pltpu.SemaphoreType.DMA((count,)),
        ],
        compiler_params=pltpu.CompilerParams(collective_id=0, has_side_effects=True, vmem_limit_bytes=48 << 20),
    )(turbulence, *consts)


def solution(mesh):
    def run(turbulence):
        n = turbulence.shape[1]
        t = tables(n, n * lax.axis_size("gx"))
        return local(turbulence, [jnp.asarray(t[k]) for k in ("wa", "wb", "sa", "ra", "g1a", "g1b", "g2a", "g2b")])

    spec = P(*AXES)
    return jax.shard_map(run, mesh=mesh, in_specs=(spec,), out_specs=spec, check_vma=False)
```

time: 103 us -> 40.9 us (0.40)
  the two profiles are of different devices: /device:TPU:15 before, /device:TPU:1 now
where the time goes in v1:
time: 40.9 us; the launch traced here: 40.3 us
  Pallas kernels  31.7 us (78%)
  local copies, waits for them, and re-layouts  8.62 us (21%)
    pallas_call x1, Pallas kernels, local(): pl.pallas_call(kernel, out_shape=jax.ShapeDtypeStruct(turbulence.shape, f...  31.7 us
    unnamed x19, local copies, waits for them, and re-layouts  8.62 us

profile of v1, /device:TPU:1, one launch (start us, length us, event | category | flops | bytes accessed | tf_op | source)
XLA Modules:
  0.0 40.3 jit_solution(9150511453102580475)
XLA Ops:
  0.0 0.0 copy-start
  0.0 1.2 %copy-done = f32[16,128,128]{2,1,0:T(8,128)S(1)} copy-done((f32[16,128,128]{2,1,0:T(8,128)S(1)}, f32[16,128,128]{2,1,0:T(8,128)}, u32[]{:S(2)}) %copy-start) | copy-done | bytes 1048600
  1.2 0.0 copy-start.1
  1.2 0.9 %copy-done.1 = bf16[256,256]{1,0:T(8,128)(2,1)S(1)} copy-done((bf16[256,256]{1,0:T(8,128)(2,1)S(1)}, bf16[256,256]{1,0:T(8,128)(2,1)}, u32[]{:S(2)}) %copy-start.1) | copy-done | bytes 131096
  2.1 0.0 copy-start.2
  2.1 0.9 %copy-done.2 = bf16[144,256]{1,0:T(8,128)(2,1)S(1)} copy-done((bf16[144,256]{1,0:T(8,128)(2,1)S(1)}, bf16[144,256]{1,0:T(8,128)(2,1)}, u32[]{:S(2)}) %copy-start.2) | copy-done | bytes 73752
  3.0 0.0 copy-start.3
  3.0 0.8 %copy-done.3 = bf16[128,256]{1,0:T(8,128)(2,1)S(1)} copy-done((bf16[128,256]{1,0:T(8,128)(2,1)S(1)}, bf16[128,256]{1,0:T(8,128)(2,1)}, u32[]{:S(2)}) %copy-start.3) | copy-done | bytes 65560
  3.9 0.0 copy-start.4
  3.9 0.8 %copy-done.4 = bf16[128,256]{1,0:T(8,128)(2,1)S(1)} copy-done((bf16[128,256]{1,0:T(8,128)(2,1)S(1)}, bf16[128,256]{1,0:T(8,128)(2,1)}, u32[]{:S(2)}) %copy-start.4) | copy-done | bytes 65560
  4.7 0.0 copy-start.5
  4.7 0.8 %copy-done.5 = bf16[144,128]{1,0:T(8,128)(2,1)S(1)} copy-done((bf16[144,128]{1,0:T(8,128)(2,1)S(1)}, bf16[144,128]{1,0:T(8,128)(2,1)}, u32[]{:S(2)}) %copy-start.5) | copy-done | bytes 36888
  5.5 0.0 copy-start.6
  5.5 0.8 %copy-done.6 = bf16[128,128]{1,0:T(8,128)(2,1)S(1)} copy-done((bf16[128,128]{1,0:T(8,128)(2,1)S(1)}, bf16[128,128]{1,0:T(8,128)(2,1)}, u32[]{:S(2)}) %copy-start.6) | copy-done | bytes 32792
  6.2 0.0 copy-start.7
  6.2 0.7 %copy-done.7 = bf16[48,256]{1,0:T(8,128)(2,1)S(1)} copy-done((bf16[48,256]{1,0:T(8,128)(2,1)S(1)}, bf16[48,256]{1,0:T(8,128)(2,1)}, u32[]{:S(2)}) %copy-start.7) | copy-done | bytes 24600
  7.0 0.0 copy-start.8
  7.0 0.7 %copy-done.8 = bf16[32,128]{1,0:T(8,128)(2,1)S(1)} copy-done((bf16[32,128]{1,0:T(8,128)(2,1)S(1)}, bf16[32,128]{1,0:T(8,128)(2,1)}, u32[]{:S(2)}) %copy-start.8) | copy-done | bytes 8216
  7.7 31.7 %shard_map.91 = f32[16,128,128]{2,1,0:T(8,128)S(1)} custom-call(f32[16,128,128]{2,1,0:T(8,128)S(1)} %copy-done, bf16[256,256]{1,0:T(8,128)(2,1)S(1)} %copy-done.1, bf16[128,256]{1,0:T(8,128)(2,1)S(1)} %copy-done.4, bf16[32,128]{1,0:T(8,128)(2,1)S(1)} %copy-done.8, bf16[48,256]{1,0:T(8,128)(2,1)S(1)} %copy-done.7, bf16[144,256]{1,0:T(8,128)(2,1)S(1)} %copy-done.2, ...), custom_call_target="tpu_custom_call" | custom-call | tf_op jit(solution)/shard_map/pallas_call | solution.py:350
  39.4 1.0 %copy.11 = f32[16,128,128]{2,1,0:T(8,128)} copy(f32[16,128,128]{2,1,0:T(8,128)S(1)} %shard_map.91) | data formatting | bytes 2097152
Async XLA Ops:
  0.0 1.2 %copy-start = (f32[16,128,128]{2,1,0:T(8,128)S(1)}, f32[16,128,128]{2,1,0:T(8,128)}, u32[]{:S(2)}) copy-start(f32[16,128,128]{2,1,0:T(8,128)} %x.1) | copy-start | bytes 3145732
  1.2 0.9 %copy-start.1 = (bf16[256,256]{1,0:T(8,128)(2,1)S(1)}, bf16[256,256]{1,0:T(8,128)(2,1)}, u32[]{:S(2)}) copy-start(bf16[256,256]{1,0:T(8,128)(2,1)} %constant.16.clone.wa) | copy-start | bytes 393220
  2.1 0.9 %copy-start.2 = (bf16[144,256]{1,0:T(8,128)(2,1)S(1)}, bf16[144,256]{1,0:T(8,128)(2,1)}, u32[]{:S(2)}) copy-start(bf16[144,256]{1,0:T(8,128)(2,1)} %constant.20.clone.g1a) | copy-start | bytes 221188
  3.0 0.8 %copy-start.3 = (bf16[128,256]{1,0:T(8,128)(2,1)S(1)}, bf16[128,256]{1,0:T(8,128)(2,1)}, u32[]{:S(2)}) copy-start(bf16[128,256]{1,0:T(8,128)(2,1)} %constant.22.clone.g2a) | copy-start | bytes 196612
  3.9 0.8 %copy-start.4 = (bf16[128,256]{1,0:T(8,128)(2,1)S(1)}, bf16[128,256]{1,0:T(8,128)(2,1)}, u32[]{:S(2)}) copy-start(bf16[128,256]{1,0:T(8,128)(2,1)} %constant.17.clone.wb) | copy-start | bytes 196612
  4.7 0.8 %copy-start.5 = (bf16[144,128]{1,0:T(8,128)(2,1)S(1)}, bf16[144,128]{1,0:T(8,128)(2,1)}, u32[]{:S(2)}) copy-start(bf16[144,128]{1,0:T(8,128)(2,1)} %constant.21.clone.g1b) | copy-start | bytes 110596
  5.5 0.8 %copy-start.6 = (bf16[128,128]{1,0:T(8,128)(2,1)S(1)}, bf16[128,128]{1,0:T(8,128)(2,1)}, u32[]{:S(2)}) copy-start(bf16[128,128]{1,0:T(8,128)(2,1)} %constant.23.clone.g2b) | copy-start | bytes 98308
  6.2 0.7 %copy-start.7 = (bf16[48,256]{1,0:T(8,128)(2,1)S(1)}, bf16[48,256]{1,0:T(8,128)(2,1)}, u32[]{:S(2)}) copy-start(bf16[48,256]{1,0:T(8,128)(2,1)} %constant.19.clone.ra) | copy-start | bytes 73732
  7.0 0.7 %copy-start.8 = (bf16[32,128]{1,0:T(8,128)(2,1)S(1)}, bf16[32,128]{1,0:T(8,128)(2,1)}, u32[]{:S(2)}) copy-start(bf16[32,128]{1,0:T(8,128)(2,1)} %constant.18.clone.sa) | copy-start | bytes 24580

commit v2 on v1

--- a/solution.py
+++ b/solution.py
@@ -142,11 +142,24 @@
 
 
 def kernel(
-    x, wa, wb, sa, ra, g1a, g1b, g2a, g2b, out,
+    x_hbm, *rest
+):
+    tables_hbm, (out, x, *rest) = rest[:8], rest[8:]
+    tables_vmem, rest = rest[:8], rest[8:]
+    body(x_hbm, tables_hbm, out, x, tables_vmem, *rest)
+
+
+def body(
+    x_hbm, tables_hbm, out, x, tables_vmem, local_sem,
     yc, q1, q2, q3, f2, f3,
     ys, yr, xs, xr, zs, zr, ps, pr, es, er, ds, dr, cs, cr,
     send_sem, recv_sem,
 ):
+    loads = [pltpu.make_async_copy(x_hbm, x, local_sem.at[0])]
+    loads += [pltpu.make_async_copy(a, b, local_sem.at[k]) for k, (a, b) in enumerate(zip(tables_hbm, tables_vmem), 1)]
+    for load in loads:
+        load.start()
+    sa, wa, wb, ra, g1a, g1b, g2a, g2b = tables_vmem
     barrier = pltpu.get_barrier_semaphore()
     for offsets in TARGETS:
         pl.semaphore_signal(barrier, inc=1, device_id=neighbour(offsets), device_id_type=pl.DeviceIdType.MESH)
@@ -164,6 +177,10 @@
         return copy
 
     nz, nx, ny = x.shape
+
+    with jax.named_scope("load"):
+        for load in loads:
+            load.wait()
 
     v = x[...].reshape(nz * nx, ny)
     hi, lo = halo_parts(v)
@@ -350,9 +367,12 @@
     return pl.pallas_call(
         kernel,
         out_shape=jax.ShapeDtypeStruct(turbulence.shape, f32),
-        in_specs=[pl.BlockSpec(memory_space=pltpu.VMEM)] * (1 + len(consts)),
+        in_specs=[pl.BlockSpec(memory_space=pltpu.HBM)] * (1 + len(consts)),
         out_specs=pl.BlockSpec(memory_space=pltpu.VMEM),
         scratch_shapes=[
+            vmem(nz, nx, ny),
+            *[pltpu.VMEM(c.shape, c.dtype) for c in consts],
+            pltpu.SemaphoreType.DMA((1 + len(consts),)),
             vmem(nz, nx, 2 * ny), vmem(nz, 144, ny), vmem(nz, 80, ny), vmem(nz, 48, ny),
             vmem(8, 64, ny), vmem(4, 32, ny),
             *pair(2, 8, nz * nx),
@@ -366,14 +386,14 @@
             pltpu.SemaphoreType.DMA((count,)),
         ],
         compiler_params=pltpu.CompilerParams(collective_id=0, has_side_effects=True, vmem_limit_bytes=48 << 20),
-    )(turbulence, *consts)
+    )(*[pltpu.with_memory_space_constraint(a, pltpu.HBM) for a in (turbulence, *consts)])
 
 
 def solution(mesh):
     def run(turbulence):
         n = turbulence.shape[1]
         t = tables(n, n * lax.axis_size("gx"))
-        return local(turbulence, [jnp.asarray(t[k]) for k in ("wa", "wb", "sa", "ra", "g1a", "g1b", "g2a", "g2b")])
+        return local(turbulence, [jnp.asarray(t[k]) for k in ("sa", "wa", "wb", "ra", "g1a", "g1b", "g2a", "g2b")])
 
     spec = P(*AXES)
     return jax.shard_map(run, mesh=mesh, in_specs=(spec,), out_specs=spec, check_vma=False)

time: 40.9 us -> 32.8 us (0.80); the launches traced: 40.3 us -> 32.7 us
  local copies, waits for them, and re-layouts: 8.62 us -> 0.97 us
    unnamed x19 -> x1, local copies, waits for them, and re-layouts: 8.62 us -> 0.97 us
where the time goes in v2:
time: 32.8 us; the launch traced here: 32.7 us
  Pallas kernels  31.7 us (97%)
  local copies, waits for them, and re-layouts  0.97 us (3%)
    pallas_call x1, Pallas kernels, local(): pl.pallas_call(kernel, out_shape=jax.ShapeDtypeStruct(turbulence.shape, f...  31.7 us
    unnamed x1, local copies, waits for them, and re-layouts  0.97 us

profile of v2, /device:TPU:1, one launch (start us, length us, event | category | flops | bytes accessed | tf_op | source)
XLA Modules:
  0.0 32.7 jit_solution(5936331666469252235)
XLA Ops:
  0.0 31.7 %shard_map.91 = f32[16,128,128]{2,1,0:T(8,128)S(1)} custom-call(f32[16,128,128]{2,1,0:T(8,128)} %x_hbm.1, bf16[32,128]{1,0:T(8,128)(2,1)} %constant.16.clone.rest_0_, bf16[256,256]{1,0:T(8,128)(2,1)} %constant.17.clone.rest_1_, bf16[128,256]{1,0:T(8,128)(2,1)} %constant.18.clone.rest_2_, bf16[48,256]{1,0:T(8,128)(2,1)} %constant.19.clone.rest_3_, ...), custom_call_target="tpu_custom_call" | custom-call | tf_op jit(solution)/shard_map/pallas_call | solution.py:367
  31.7 1.0 %copy.11 = f32[16,128,128]{2,1,0:T(8,128)} copy(f32[16,128,128]{2,1,0:T(8,128)S(1)} %shard_map.91) | data formatting | bytes 2097152

commit v3 on v1

v3 whole, which is shorter than its diff:
```python
import functools

import jax
import jax.numpy as jnp
import ml_dtypes
import numpy as np
from jax import lax
from jax.experimental import pallas as pl
from jax.experimental.pallas import tpu as pltpu
from jax.sharding import PartitionSpec as P

ALPHA = -1.586134342059924
BETA = -0.052980118572961
GAMMA = 0.882911075530934
DELTA = 0.443506852043971
ZETA = 1.149604398860241
AXES = ("gz", "gx", "gy")
BF16 = ml_dtypes.bfloat16


def lifting_matrix(n):
    v = np.eye(n)
    s, d = v[0::2].copy(), v[1::2].copy()
    d = d + ALPHA * (s + np.roll(s, -1, 0))
    s = s + BETA * (np.roll(d, 1, 0) + d)
    d = d + GAMMA * (s + np.roll(s, -1, 0))
    s = s + DELTA * (np.roll(d, 1, 0) + d)
    out = np.zeros((n, n))
    out[0::2], out[1::2] = s * ZETA, d / ZETA
    return out


def blocks(n, total):
    m, k, out = np.eye(total), total, []
    p = total // n // 2
    for level in range(3):
        t = lifting_matrix(k) @ m
        rows = t[p * k * n // total : (p + 1) * k * n // total]
        out.append([rows[:, (p + o) * n : (p + o + 1) * n] for o in (-1, 0, 1)])
        m, k = t[0::2], k // 2
    return out


def split(m):
    hi = m.astype(np.float32).astype(BF16)
    lo = (m - hi.astype(np.float64)).astype(np.float32).astype(BF16)
    return hi, lo


def low_rank(m, rank):
    u, s, v = np.linalg.svd(m, full_matrices=False)
    return u[:, :rank] * s[:rank], v[:rank]


def tables(n, total):
    per_level = blocks(n, total)
    place = np.zeros((2 * n, n + n // 2 + n // 4))
    place[np.arange(n), np.arange(n)] = 1
    place[n + 2 * np.arange(n // 2), n + np.arange(n // 2)] = 1
    place[n + 4 * np.arange(n // 4) + 1, n + n // 2 + np.arange(n // 4)] = 1
    before, own, after = (place @ np.concatenate([lv[o] for lv in per_level]) for o in range(3))
    r_before, s_before = low_rank(before, 6)
    r_after, s_after = low_rank(after, 6)
    send = np.zeros((16, n))
    send[0:6], send[8:14] = s_before, s_after
    take = np.zeros((16, 2 * n))
    take[0:6], take[8:14] = r_before.T, r_after.T
    w_hi, w_lo = split(own.T)
    t_hi, t_lo = split(take)
    ext = [np.concatenate([lv[1], lv[0][:w], lv[2][-w:]]) for lv, w in zip(per_level, (4, 8, 8))]
    g1_hi, g1_lo = split(ext[0])
    g2_hi, g2_lo = split(np.concatenate(ext[1:]))
    return dict(
        sa=np.concatenate(split(send)),
        wa=np.concatenate([w_hi, w_hi]),
        wb=w_lo,
        g1a=np.concatenate([g1_hi, g1_hi], axis=1),
        g1b=g1_lo,
        g2a=np.concatenate([g2_hi, g2_hi], axis=1),
        g2b=g2_lo,
        ra=np.concatenate([t_hi, t_hi, t_lo]),
    )


def level2_shares(n, total):
    before, _, after = blocks(n, total)[1]
    return before @ np.linalg.pinv(before[0:3]), after @ np.linalg.pinv(after[5:8])


def add(*terms):
    total = None
    for coefficient, v in terms:
        if v is None:
            continue
        v = v if coefficient == 1 else v * coefficient
        total = v if total is None else total + v
    return total


def plus(base, coefficient, one, two):
    pair = one if two is None else two if one is None else one + two
    return add((1, base), (coefficient, pair))


def lift_zero_extended(v, lowest, highest, low_only=False):
    a, b = lowest // 2 - 2, highest // 2 + 3
    s = {i: v.get(2 * i) for i in range(a, b + 1)}
    d = {i: v.get(2 * i + 1) for i in range(a, b + 1)}
    d1 = {i: plus(d[i], ALPHA, s[i], s[i + 1]) for i in range(a, b)}
    s1 = {i: plus(s[i], BETA, d1[i - 1], d1[i]) for i in range(a + 1, b)}
    d2 = {i: plus(d1[i], GAMMA, s1[i], s1[i + 1]) for i in range(a + 1, b - 1)}
    s2 = {i: plus(s1[i], DELTA, d2[i - 1], d2[i]) for i in range(a + 2, b - 1)}
    out = {}
    for i in range(a + 2, b - 1):
        for k, part, scale in ((2 * i, s2[i], ZETA), (2 * i + 1, d2[i], 1 / ZETA)):
            if lowest <= k <= highest and part is not None and not (low_only and k % 2):
                out[k] = part * scale
    return out, d1, s1


def halo_parts(v):
    bf = jnp.bfloat16
    hi = v.astype(bf)
    return hi, (v - hi.astype(jnp.float32)).astype(bf)


def dot(a, b, dims=((1,), (0,))):
    return lax.dot_general(a, b, (dims, ((), ())), preferred_element_type=jnp.float32)


def neighbour(offsets):
    return {
        axis: lax.rem(lax.axis_index(axis) + (o + lax.axis_size(axis)), lax.axis_size(axis))
        for axis, o in zip(AXES, offsets)
        if o
    }


SIDES = (1, -1)
TARGETS = (
    [(0, 0, c) for c in SIDES]
    + [(0, b, 0) for b in SIDES]
    + [(a, b, 0) for a in SIDES for b in (0, 1, -1)]
    + [(2 * a, b, 0) for a in SIDES for b in (0, 1, -1)]
)


def kernel(shares, x_hbm, *refs):
    tables_hbm, out, x, tables_vmem, rest = refs[:8], refs[8], refs[9], refs[10:18], refs[18:]
    (
        yc, q1, q2, q3, f2, f3, xc, ec,
        ys, yr, xs, xr, zs, zr, ts, tr, ps, pr, es, er, ds, dr, cs, cr,
        load_sem, send_sem, recv_sem,
    ) = rest
    nz, nx, ny = x.shape
    f32 = jnp.float32

    loads = [pltpu.make_async_copy(x_hbm, x, load_sem.at[0])]
    loads += [pltpu.make_async_copy(a, b, load_sem.at[k]) for k, (a, b) in enumerate(zip(tables_hbm, tables_vmem), 1)]
    for load in loads:
        load.start()
    sa, wa, wb, g1a, g1b, g2a, g2b, ra = tables_vmem
    barrier = pltpu.get_barrier_semaphore()
    for offsets in TARGETS:
        pl.semaphore_signal(barrier, inc=1, device_id=neighbour(offsets), device_id_type=pl.DeviceIdType.MESH)

    copies = []

    def send(source, target, offsets):
        k = len(copies)
        copy = pltpu.make_async_remote_copy(
            source, target, send_sem.at[k], recv_sem.at[k],
            device_id=neighbour(offsets), device_id_type=pl.DeviceIdType.MESH,
        )
        copies.append(copy)
        copy.start()
        return copy

    row = lax.broadcasted_iota(jnp.int32, (8, 128), 0)
    lane = lax.broadcasted_iota(jnp.int32, (8, 128), 1)

    def pack_rows(one, two, side):
        if side == 0:
            return jnp.where(row < 4, one, pltpu.roll(two, 4, 0))
        return jnp.where(row < 4, pltpu.roll(one, 4, 0), two)

    def unpack_rows(packed, second, side):
        v = packed if second == side else pltpu.roll(packed, 4, 0)
        return jnp.where((row < 4) == (side == 0), v, 0.0)

    def pack2(one, two):
        two = jnp.zeros_like(one) if two is None else pltpu.roll(two, 1, 1)
        return jnp.where(lane % 2 == 0, one, two)

    def pack4(parts):
        total = parts[0]
        for k, part in enumerate(parts[1:], 1):
            total = jnp.where(lane % 4 == (1 + k) % 4, pltpu.roll(part, k, 1), total)
        return total

    def shift(v, k):
        return pltpu.roll(v, 128 - k, 1) if k else v

    def lift_level1(v):
        o, d1, s1 = lift_zero_extended(v, 0, nz - 1)
        return o, ((d1[nz // 2 - 1], s1[nz // 2 - 1]), (v[0], v[0] + BETA * d1[0]))

    def expand(h, lanes):
        hi, lo = halo_parts(h)
        return dot(jnp.concatenate([hi, lo, hi], axis=0), ra[:, lanes], ((0,), (0,)))

    level1, deeper = slice(0, 128), slice(128, 256)

    with jax.named_scope("load"):
        loads[0].wait()
        loads[1].wait()

    with jax.named_scope("ymsg"):
        hi, lo = halo_parts(x[...].reshape(nz * nx, ny))
        first = dot(sa[...], hi, ((1,), (1,)))
        second = dot(sa[0:16], lo, ((1,), (1,)))
        message = first[0:16] + first[16:32] + second
        for z in range(nz):
            for c in range(2):
                ys[c, z] = message[8 * c : 8 * c + 8, z * nx : (z + 1) * nx]
    with jax.named_scope("barw"):
        pl.semaphore_wait(barrier, len(TARGETS))
        y_copies = [send(ys.at[k], yr.at[k], (0, 0, c)) for k, c in enumerate(SIDES)]

    with jax.named_scope("ycent"):
        for load in loads[2:]:
            load.wait()
        for z in range(nz):
            hi, lo = halo_parts(x[z])
            yc[z] = dot(jnp.concatenate([hi, lo], axis=1), wa[...]) + dot(hi, wb[...])
    with jax.named_scope("x1"):
        for z in range(nz):
            hi, lo = halo_parts(yc[z, :, level1])
            q1[z] = dot(g1a[...], jnp.concatenate([hi, lo], axis=0)) + dot(g1b[...], hi)
    with jax.named_scope("z1"):
        for tile in range(17):
            rows = slice(8 * tile, 8 * tile + 8)
            o, pairs = lift_level1({k: q1[k, rows] for k in range(nz)})
            for k in range(nz):
                if tile < 16:
                    out[k, rows] = o[k]
                else:
                    xc[k] = o[k]
            for a in range(2):
                for r in range(2):
                    if tile < 16:
                        zs[a, r, rows] = pairs[a][r]
                    else:
                        ec[a, r] = pairs[a][r]
        late = [send(zs.at[a], zr.at[a], (s, 0, 0)) for a, s in enumerate(SIDES)]
    with jax.named_scope("x2"):
        for z in range(nz):
            hi, lo = halo_parts(yc[z, :, deeper])
            q = dot(g2a[...], jnp.concatenate([hi, lo], axis=0)) + dot(g2b[...], hi)
            q2[z] = q[0:80]
            q3[z] = q[80:128]

    with jax.named_scope("ywait"):
        for copy in y_copies:
            copy.wait_recv()

    with jax.named_scope("halo"):
        h = jnp.concatenate([yr[0], yr[1]], axis=1).reshape(nz * 16, nx)
        hi, lo = halo_parts(h)
        both = jnp.concatenate([hi, lo], axis=1)
        rhs = ((1,), (1,))
        t1 = (dot(both, g1a[...], rhs) + dot(hi, g1b[...], rhs)).reshape(nz, 16, 136)
        t2 = (dot(both, g2a[...], rhs) + dot(hi, g2b[...], rhs)).reshape(nz, 16, 128)
        t1, t1_pairs = lift_level1({k: t1[k] for k in range(nz)})
        for a in range(2):
            for r in range(2):
                ts[a, r] = t1_pairs[a][r][:, 0:nx]
        for a, s in enumerate(SIDES):
            late.append(send(ts.at[a], tr.at[a], (s, 0, 0)))
    with jax.named_scope("q23"):
        for z in range(nz):
            q = expand(t2[z], deeper)
            q2[z] += q[0:80]
            q3[z] += q[80:128]

    with jax.named_scope("z23"):
        for tile in (8, 9, 0, 1, 2, 3, 4, 5, 6, 7):
            rows = slice(8 * tile, 8 * tile + 8)
            c2, _, _ = lift_zero_extended({k: q2[k, rows] for k in range(nz)}, -4, nz + 3, True)
            o, _, _ = lift_zero_extended({k // 2: w for k, w in c2.items()}, -3, 10)
            if tile < 8:
                for k in range(8):
                    f2[k, rows] = o[k]
            else:
                for k in range(4):
                    xs[tile - 8, 8 + k] = pack2(o[2 * k], o[2 * k + 1])
            for a, (one, two, three) in enumerate(((8, 9, 10), (-3, -2, -1))):
                for r, packed in enumerate((pack2(o[one], o[two]), pack2(o[three], None))):
                    if tile < 8:
                        ps[a, 64 * r + 8 * tile : 64 * r + 8 * tile + 8] = packed
                    else:
                        es[2 * a + tile - 8, 1 + r] = packed
        zero = jnp.zeros((8, 128), f32)
        for tile in range(6):
            rows = slice(8 * tile, 8 * tile + 8)
            c2, _, _ = lift_zero_extended({k: q3[k, rows] for k in range(nz)}, -4, nz + 3, True)
            c3, _, _ = lift_zero_extended({k // 2: w for k, w in c2.items()}, -6, 12, True)
            o, _, _ = lift_zero_extended({k // 2: w for k, w in c3.items()}, -6, 10)
            if tile < 4:
                for k in range(4):
                    f3[k, rows] = o[k]
            else:
                xs[tile - 4, 12] = pack4([o[0], o[1], o[2], o[3]])
            near = (pack4([o[4], o[5], o[6], o[7]]), pack4([o[-4], o[-3], o[-2], o[-1]]))
            far = (pack4([o[8], o[9], o[10], zero]), pack4([zero, zero, o[-6], o[-5]]))
            for a in range(2):
                if tile < 4:
                    ps[a, 128 + 8 * tile : 136 + 8 * tile] = near[a]
                    ds[a, rows] = far[a]
                else:
                    es[2 * a + tile - 4, 3] = near[a]
                    cs[2 * a + tile - 4] = far[a]
        for a, s in enumerate(SIDES):
            late.append(send(ds.at[a], dr.at[a], (2 * s, 0, 0)))
            late.append(send(ps.at[a], pr.at[a], (s, 0, 0)))
            for b, t in enumerate(SIDES):
                late.append(send(cs.at[2 * a + b], cr.at[2 * a + b], (2 * s, t, 0)))

    with jax.named_scope("xs"):
        full = [xc[k] + expand(t1[k][:, nx : nx + 8], level1) for k in range(nz)]
        for k in range(nz // 2):
            for b in range(2):
                xs[b, k] = pack_rows(full[2 * k], full[2 * k + 1], b)
        for a in range(2):
            full = [ec[a, r] + expand(t1_pairs[a][r][:, nx : nx + 8], level1) for r in range(2)]
            for b in range(2):
                es[2 * a + b, 0] = pack_rows(full[0], full[1], b)
        for b, t in enumerate(SIDES):
            late.append(send(xs.at[b], xr.at[b], (0, t, 0)))
            for a, s in enumerate(SIDES):
                late.append(send(es.at[2 * a + b], er.at[2 * a + b], (s, t, 0)))

    with jax.named_scope("own1"):
        for k in range(nz):
            out[k] += expand(t1[k][:, 0:nx], level1)

    with jax.named_scope("wait2"):
        for copy in late:
            copy.wait_recv()

    with jax.named_scope("edges"):
        for a in range(2):
            for r in range(2):
                zr[a, r] += expand(tr[a, r], level1)
            for b, (r1, r2, r3) in enumerate(((0, 0, 0), (nx - 8, nx // 2 - 8, nx // 4 - 8))):
                e = 2 * a + b
                for r in range(2):
                    zr[a, r, r1 : r1 + 8] += unpack_rows(er[e, 0], r, b)
                    pr[a, 64 * r + r2 : 64 * r + r2 + 8] += er[e, 1 + r]
                pr[a, 128 + r3 : 136 + r3] += er[e, 3]
                dr[a, r3 : r3 + 8] += cr[e]

    with jax.named_scope("xfaces"):
        for b, (r1, r2, r3) in enumerate(((0, 0, 0), (nx - 8, nx // 2 - 8, nx // 4 - 8))):
            for k in range(16):
                out[k, r1 : r1 + 8] += unpack_rows(xr[b, k // 2], k % 2, b)
            for k in range(8):
                f2[k, r2 : r2 + 8] += shift(xr[b, 8 + k // 2], k % 2)
            for k in range(4):
                f3[k, r3 : r3 + 8] += shift(xr[b, 12], k)

    with jax.named_scope("zfaces"):
        for tile in range(16):
            rows = slice(8 * tile, 8 * tile + 8)
            one, two = zr[0, 0, rows], zr[0, 1, rows]
            s10 = BETA * one
            d2m = one + GAMMA * (two + s10)
            d20 = GAMMA * s10
            s20 = s10 + DELTA * (d2m + d20)
            out[0, rows] += ZETA * s20
            out[1, rows] += (1 / ZETA) * d20
            out[2, rows] += (ZETA * DELTA) * d20
            one, two = zr[1, 0, rows], zr[1, 1, rows]
            d17 = ALPHA * one
            s17 = BETA * d17
            d27 = d17 + GAMMA * (s17 + two + s17)
            d26 = GAMMA * s17
            s27 = s17 + DELTA * (d26 + d27)
            out[nz - 4, rows] += (ZETA * DELTA) * d26
            out[nz - 3, rows] += (1 / ZETA) * d26
            out[nz - 2, rows] += ZETA * s27
            out[nz - 1, rows] += (1 / ZETA) * d27

    with jax.named_scope("final"):
        lane3 = lax.broadcasted_iota(jnp.int32, (32, 128), 1)
        lane2 = lax.broadcasted_iota(jnp.int32, (64, 128), 1)
        parts = []
        for a in range(2):
            first, second = pr[a, 0:64], pr[a, 64:128]
            parts.append((first, shift(first, 1), second))
        deep = pr[0, 128:160] + pr[1, 128:160] + dr[0] + dr[1]
        for k in range(8):
            total = f2[k]
            for a in range(2):
                total = add((1, total), *[(float(shares[a][k, r]), parts[a][r]) for r in range(3) if abs(shares[a][k, r]) > 1e-12])
            f2[k] = total
            if k % 2 == 0:
                j = k // 2
                even = pl.ds(0, 32, 2)
                f2[k, even, :] = jnp.where(lane3 % 4 == 0, shift(f3[j], 1) + shift(deep, 1 + j), f2[k, even, :])
            even = pl.ds(0, 64, 2)
            out[2 * k, even, :] = jnp.where(lane2 % 2 == 0, f2[k], out[2 * k, even, :])

    with jax.named_scope("sendwait"):
        for copy in copies:
            copy.wait_send()


def local(turbulence, consts, shares):
    nz, nx, ny = turbulence.shape
    f32 = jnp.float32
    vmem = lambda *shape: pltpu.VMEM(shape, f32)
    pair = lambda *shape: [vmem(*shape), vmem(*shape)]
    count = 20
    return pl.pallas_call(
        functools.partial(kernel, shares),
        out_shape=jax.ShapeDtypeStruct(turbulence.shape, f32),
        in_specs=[pl.BlockSpec(memory_space=pltpu.HBM)] * (1 + len(consts)),
        out_specs=pl.BlockSpec(memory_space=pltpu.VMEM),
        scratch_shapes=[
            vmem(nz, nx, ny),
            *[pltpu.VMEM(c.shape, c.dtype) for c in consts],
            vmem(nz, nx, 2 * ny), vmem(nz, 136, ny), vmem(nz, 80, ny), vmem(nz, 48, ny),
            vmem(8, 64, ny), vmem(4, 32, ny),
            vmem(nz, 8, ny), vmem(2, 2, 8, ny),
            *pair(2, nz, 8, nx),
            *pair(2, 13, 8, ny),
            *pair(2, 2, nx, ny),
            *pair(2, 2, 16, nx),
            *pair(2, 160, ny),
            *pair(4, 4, 8, ny),
            *pair(2, 32, ny),
            *pair(4, 8, ny),
            pltpu.SemaphoreType.DMA((1 + len(consts),)),
            pltpu.SemaphoreType.DMA((count,)),
            pltpu.SemaphoreType.DMA((count,)),
        ],
        compiler_params=pltpu.CompilerParams(collective_id=0, has_side_effects=True, vmem_limit_bytes=48 << 20),
    )(*[pltpu.with_memory_space_constraint(a, pltpu.HBM) for a in (turbulence, *consts)])


def solution(mesh):
    def run(turbulence):
        nz, n, _ = turbulence.shape
        t = tables(n, n * lax.axis_size("gx"))
        names = ("sa", "wa", "wb", "g1a", "g1b", "g2a", "g2b", "ra")
        return local(turbulence, [jnp.asarray(t[k]) for k in names], level2_shares(nz, nz * lax.axis_size("gz")))

    spec = P(*AXES)
    return jax.shard_map(run, mesh=mesh, in_specs=(spec,), out_specs=spec, check_vma=False)
```

time: 40.9 us -> 26.5 us (0.65); the launches traced: 40.3 us -> 26.4 us
  local copies, waits for them, and re-layouts: 8.62 us -> 0.97 us
  Pallas kernels: 31.7 us -> 25.4 us
    unnamed x19 -> x1, local copies, waits for them, and re-layouts: 8.62 us -> 0.97 us
    pallas_call x1, Pallas kernels: 31.7 us -> 25.4 us  [local(): pl.pallas_call(functools.partial(kernel, shares), out_shape=jax.ShapeDtyp...]
where the time goes in v3:
time: 26.5 us; the launch traced here: 26.4 us
  Pallas kernels  25.4 us (96%)
  local copies, waits for them, and re-layouts  0.97 us (4%)
    pallas_call x1, Pallas kernels, local(): pl.pallas_call(functools.partial(kernel, shares), out_shape=jax.ShapeDtyp...  25.4 us
    unnamed x1, local copies, waits for them, and re-layouts  0.97 us

profile of v3, /device:TPU:1, one launch (start us, length us, event | category | flops | bytes accessed | tf_op | source)
XLA Modules:
  0.0 26.4 jit_solution(14983052152282402503)
XLA Ops:
  0.0 25.4 %shard_map.91 = f32[16,128,128]{2,1,0:T(8,128)S(1)} custom-call(f32[16,128,128]{2,1,0:T(8,128)} %x_hbm.1, bf16[32,128]{1,0:T(8,128)(2,1)} %constant.16.clone.refs_0_, bf16[256,256]{1,0:T(8,128)(2,1)} %constant.17.clone.refs_1_, bf16[128,256]{1,0:T(8,128)(2,1)} %constant.18.clone.refs_2_, bf16[136,256]{1,0:T(8,128)(2,1)} %constant.19.clone.refs_3_, ...), custom_call_target="tpu_custom_call" | custom-call | tf_op jit(solution)/shard_map/pallas_call | solution.py:425
  25.4 1.0 %copy.11 = f32[16,128,128]{2,1,0:T(8,128)} copy(f32[16,128,128]{2,1,0:T(8,128)S(1)} %shard_map.91) | data formatting | bytes 2097152

commit v4 on v3

--- a/solution.py
+++ b/solution.py
@@ -47,9 +47,13 @@
     return hi, lo
 
 
-def low_rank(m, rank):
-    u, s, v = np.linalg.svd(m, full_matrices=False)
-    return u[:, :rank] * s[:rank], v[:rank]
+def low_rank(m, first, rank, rank_first):
+    v = np.linalg.svd(m[:first])[2][:rank_first]
+    rest = np.linalg.svd(m - m @ v.T @ v)[2][: rank - rank_first]
+    v = np.concatenate([v, rest])
+    left = m @ v.T
+    left[:first, rank_first:] = 0
+    return left, v
 
 
 def tables(n, total):
@@ -59,8 +63,8 @@
     place[n + 2 * np.arange(n // 2), n + np.arange(n // 2)] = 1
     place[n + 4 * np.arange(n // 4) + 1, n + n // 2 + np.arange(n // 4)] = 1
     before, own, after = (place @ np.concatenate([lv[o] for lv in per_level]) for o in range(3))
-    r_before, s_before = low_rank(before, 6)
-    r_after, s_after = low_rank(after, 6)
+    r_before, s_before = low_rank(before, n, 6, 2)
+    r_after, s_after = low_rank(after, n, 6, 2)
     send = np.zeros((16, n))
     send[0:6], send[8:14] = s_before, s_after
     take = np.zeros((16, 2 * n))
@@ -87,6 +91,16 @@
     return before @ np.linalg.pinv(before[0:3]), after @ np.linalg.pinv(after[5:8])
 
 
+def level3_shares(n, total):
+    m = np.eye(total)
+    for k in (total, total // 2, total // 4):
+        rows = lifting_matrix(k) @ m
+        m = rows[0::2]
+    p = total // n // 2
+    far = rows[p * n // 4 : (p + 1) * n // 4, (p - 2) * n : (p - 1) * n]
+    return (far @ np.linalg.pinv(far[0:2]))[2]
+
+
 def add(*terms):
     total = None
     for coefficient, v in terms:
@@ -138,14 +152,13 @@
 
 SIDES = (1, -1)
 TARGETS = (
-    [(0, 0, c) for c in SIDES]
-    + [(0, b, 0) for b in SIDES]
-    + [(a, b, 0) for a in SIDES for b in (0, 1, -1)]
-    + [(2 * a, b, 0) for a in SIDES for b in (0, 1, -1)]
+    [(a, b, 0) for a in (2, -2, 1, -1, 0) for b in SIDES]
+    + [(a, 0, 0) for a in (2, -2, 1, -1)]
+    + [(0, 0, c) for c in SIDES]
 )
 
 
-def kernel(shares, x_hbm, *refs):
+def kernel(shares, far_share, x_hbm, *refs):
     tables_hbm, out, x, tables_vmem, rest = refs[:8], refs[8], refs[9], refs[10:18], refs[18:]
     (
         yc, q1, q2, q3, f2, f3, xc, ec,
@@ -157,12 +170,14 @@
 
     loads = [pltpu.make_async_copy(x_hbm, x, load_sem.at[0])]
     loads += [pltpu.make_async_copy(a, b, load_sem.at[k]) for k, (a, b) in enumerate(zip(tables_hbm, tables_vmem), 1)]
-    for load in loads:
+    for load in loads[:2]:
         load.start()
     sa, wa, wb, g1a, g1b, g2a, g2b, ra = tables_vmem
     barrier = pltpu.get_barrier_semaphore()
     for offsets in TARGETS:
         pl.semaphore_signal(barrier, inc=1, device_id=neighbour(offsets), device_id_type=pl.DeviceIdType.MESH)
+    for load in loads[2:]:
+        load.start()
 
     copies = []
 
@@ -224,8 +239,17 @@
             for c in range(2):
                 ys[c, z] = message[8 * c : 8 * c + 8, z * nx : (z + 1) * nx]
     with jax.named_scope("barw"):
+        for tile in range(16):
+            rows = slice(8 * tile, 8 * tile + 8)
+            v = {k: x[k, rows] for k in (0, 1, 2, nz - 4, nz - 3, nz - 2, nz - 1)}
+            last = v[nz - 1] + ALPHA * v[nz - 2]
+            zs[0, 0, rows] = last
+            zs[0, 1, rows] = v[nz - 2] + BETA * (v[nz - 3] + ALPHA * (v[nz - 4] + v[nz - 2]) + last)
+            zs[1, 0, rows] = v[0]
+            zs[1, 1, rows] = v[0] + BETA * (v[1] + ALPHA * (v[0] + v[2]))
         pl.semaphore_wait(barrier, len(TARGETS))
         y_copies = [send(ys.at[k], yr.at[k], (0, 0, c)) for k, c in enumerate(SIDES)]
+        z_copies = [send(zs.at[a], zr.at[a], (s, 0, 0)) for a, s in enumerate(SIDES)]
 
     with jax.named_scope("ycent"):
         for load in loads[2:]:
@@ -246,13 +270,11 @@
                     out[k, rows] = o[k]
                 else:
                     xc[k] = o[k]
-            for a in range(2):
-                for r in range(2):
-                    if tile < 16:
-                        zs[a, r, rows] = pairs[a][r]
-                    else:
+            if tile == 16:
+                for a in range(2):
+                    for r in range(2):
                         ec[a, r] = pairs[a][r]
-        late = [send(zs.at[a], zr.at[a], (s, 0, 0)) for a, s in enumerate(SIDES)]
+        late = []
     with jax.named_scope("x2"):
         for z in range(nz):
             hi, lo = halo_parts(yc[z, :, deeper])
@@ -273,8 +295,9 @@
         t2 = (dot(both, g2a[...], rhs) + dot(hi, g2b[...], rhs)).reshape(nz, 16, 128)
         t1, t1_pairs = lift_level1({k: t1[k] for k in range(nz)})
         for a in range(2):
-            for r in range(2):
-                ts[a, r] = t1_pairs[a][r][:, 0:nx]
+            (one, two), (three, four) = ((t[0:8, 0:nx], t[8:16, 0:nx]) for t in t1_pairs[a])
+            second, fourth = jnp.where(row < 2, one, pltpu.roll(two, 2, 0)), jnp.where(row < 2, three, pltpu.roll(four, 2, 0))
+            ts[a] = jnp.where(row < 4, second, pltpu.roll(fourth, 4, 0))
         for a, s in enumerate(SIDES):
             late.append(send(ts.at[a], tr.at[a], (s, 0, 0)))
     with jax.named_scope("q23"):
@@ -300,7 +323,7 @@
                         ps[a, 64 * r + 8 * tile : 64 * r + 8 * tile + 8] = packed
                     else:
                         es[2 * a + tile - 8, 1 + r] = packed
-        zero = jnp.zeros((8, 128), f32)
+        kept = {}
         for tile in range(6):
             rows = slice(8 * tile, 8 * tile + 8)
             c2, _, _ = lift_zero_extended({k: q3[k, rows] for k in range(nz)}, -4, nz + 3, True)
@@ -311,15 +334,22 @@
                     f3[k, rows] = o[k]
             else:
                 xs[tile - 4, 12] = pack4([o[0], o[1], o[2], o[3]])
-            near = (pack4([o[4], o[5], o[6], o[7]]), pack4([o[-4], o[-3], o[-2], o[-1]]))
-            far = (pack4([o[8], o[9], o[10], zero]), pack4([zero, zero, o[-6], o[-5]]))
+            near = ((o[4], o[5], o[6], o[7]), (o[-4], o[-3], o[-2], o[-1]))
+            far = ((o[8], o[9]), (o[-6], o[-5]))
             for a in range(2):
                 if tile < 4:
-                    ps[a, 128 + 8 * tile : 136 + 8 * tile] = near[a]
-                    ds[a, rows] = far[a]
+                    for half in range(2):
+                        at = slice(64 + 32 * half + 8 * tile, 72 + 32 * half + 8 * tile)
+                        one, two = near[a][2 * half], near[a][2 * half + 1]
+                        odd = jnp.where(lane % 4 == 1, one, pltpu.roll(two, 2, 1))
+                        ps[a, at] = jnp.where(lane % 2 == 0, ps[a, at], odd)
+                    if tile < 2:
+                        kept[a, tile] = far[a]
+                    else:
+                        ds[a, 8 * tile - 16 : 8 * tile - 8] = pack4([*kept[a, tile - 2], *far[a]])
                 else:
-                    es[2 * a + tile - 4, 3] = near[a]
-                    cs[2 * a + tile - 4] = far[a]
+                    es[2 * a + tile - 4, 3] = pack4(near[a])
+                    cs[2 * a + tile - 4] = pack4([*far[a], *far[a]])
         for a, s in enumerate(SIDES):
             late.append(send(ds.at[a], dr.at[a], (2 * s, 0, 0)))
             late.append(send(ps.at[a], pr.at[a], (s, 0, 0)))
@@ -344,21 +374,44 @@
         for k in range(nz):
             out[k] += expand(t1[k][:, 0:nx], level1)
 
+    with jax.named_scope("zraw"):
+        for copy in z_copies:
+            copy.wait_recv()
+        for a in range(2):
+            for r in range(2):
+                hi, lo = halo_parts(zr[a, r])
+                y = dot(jnp.concatenate([hi, lo], axis=1), wa[:, level1]) + dot(hi, wb[:, level1])
+                hi, lo = halo_parts(y)
+                zr[a, r] = dot(g1a[0:nx], jnp.concatenate([hi, lo], axis=0)) + dot(g1b[0:nx], hi)
+
     with jax.named_scope("wait2"):
         for copy in late:
             copy.wait_recv()
 
+    def take_far(a, rows, v, first):
+        one, two = shift(v, first), shift(v, first + 1)
+        if a == 0:
+            f3[0, rows] += one
+            f3[1, rows] += two
+            f3[2, rows] += float(far_share[0]) * one + float(far_share[1]) * two
+        else:
+            f3[2, rows] += one
+            f3[3, rows] += two
+
     with jax.named_scope("edges"):
         for a in range(2):
             for r in range(2):
-                zr[a, r] += expand(tr[a, r], level1)
+                quad = pltpu.roll(tr[a], 4, 0) if r else tr[a]
+                quad = [jnp.where(row < 2, pltpu.roll(quad, 6, 0) if c else quad, 0.0) for c in range(2)]
+                zr[a, r] += expand(jnp.concatenate(quad, axis=0), level1)
             for b, (r1, r2, r3) in enumerate(((0, 0, 0), (nx - 8, nx // 2 - 8, nx // 4 - 8))):
                 e = 2 * a + b
                 for r in range(2):
                     zr[a, r, r1 : r1 + 8] += unpack_rows(er[e, 0], r, b)
                     pr[a, 64 * r + r2 : 64 * r + r2 + 8] += er[e, 1 + r]
-                pr[a, 128 + r3 : 136 + r3] += er[e, 3]
-                dr[a, r3 : r3 + 8] += cr[e]
+                for j in range(4):
+                    f3[j, r3 : r3 + 8] += shift(er[e, 3], j)
+                take_far(a, slice(r3, r3 + 8), cr[e], 0)
 
     with jax.named_scope("xfaces"):
         for b, (r1, r2, r3) in enumerate(((0, 0, 0), (nx - 8, nx // 2 - 8, nx // 4 - 8))):
@@ -398,7 +451,11 @@
         for a in range(2):
             first, second = pr[a, 0:64], pr[a, 64:128]
             parts.append((first, shift(first, 1), second))
-        deep = pr[0, 128:160] + pr[1, 128:160] + dr[0] + dr[1]
+            for half in range(2):
+                for q in range(2):
+                    f3[2 * half + q] += shift(pr[a, 64 + 32 * half : 96 + 32 * half], 2 * q)
+            for half in range(2):
+                take_far(a, slice(16 * half, 16 * half + 16), dr[a], 2 * half)
         for k in range(8):
             total = f2[k]
             for a in range(2):
@@ -407,7 +464,7 @@
             if k % 2 == 0:
                 j = k // 2
                 even = pl.ds(0, 32, 2)
-                f2[k, even, :] = jnp.where(lane3 % 4 == 0, shift(f3[j], 1) + shift(deep, 1 + j), f2[k, even, :])
+                f2[k, even, :] = jnp.where(lane3 % 4 == 0, shift(f3[j], 1), f2[k, even, :])
             even = pl.ds(0, 64, 2)
             out[2 * k, even, :] = jnp.where(lane2 % 2 == 0, f2[k], out[2 * k, even, :])
 
@@ -416,14 +473,14 @@
             copy.wait_send()
 
 
-def local(turbulence, consts, shares):
+def local(turbulence, consts, shares, far_share):
     nz, nx, ny = turbulence.shape
     f32 = jnp.float32
     vmem = lambda *shape: pltpu.VMEM(shape, f32)
     pair = lambda *shape: [vmem(*shape), vmem(*shape)]
     count = 20
     return pl.pallas_call(
-        functools.partial(kernel, shares),
+        functools.partial(kernel, shares, far_share),
         out_shape=jax.ShapeDtypeStruct(turbulence.shape, f32),
         in_specs=[pl.BlockSpec(memory_space=pltpu.HBM)] * (1 + len(consts)),
         out_specs=pl.BlockSpec(memory_space=pltpu.VMEM),
@@ -436,10 +493,10 @@
             *pair(2, nz, 8, nx),
             *pair(2, 13, 8, ny),
             *pair(2, 2, nx, ny),
-            *pair(2, 2, 16, nx),
-            *pair(2, 160, ny),
+            *pair(2, 8, nx),
+            *pair(2, 128, ny),
             *pair(4, 4, 8, ny),
-            *pair(2, 32, ny),
+            *pair(2, 16, ny),
             *pair(4, 8, ny),
             pltpu.SemaphoreType.DMA((1 + len(consts),)),
             pltpu.SemaphoreType.DMA((count,)),
@@ -454,7 +511,8 @@
         nz, n, _ = turbulence.shape
         t = tables(n, n * lax.axis_size("gx"))
         names = ("sa", "wa", "wb", "g1a", "g1b", "g2a", "g2b", "ra")
-        return local(turbulence, [jnp.asarray(t[k]) for k in names], level2_shares(nz, nz * lax.axis_size("gz")))
+        along_z = nz, nz * lax.axis_size("gz")
+        return local(turbulence, [jnp.asarray(t[k]) for k in names], level2_shares(*along_z), level3_shares(*along_z))
 
     spec = P(*AXES)
     return jax.shard_map(run, mesh=mesh, in_specs=(spec,), out_specs=spec, check_vma=False)

time: 26.5 us -> 25.7 us (0.970)
  Pallas kernels: 25.4 us -> 24.6 us
    pallas_call x1, Pallas kernels: 25.4 us -> 24.6 us  [local(): pl.pallas_call(functools.partial(kernel, shares, far_share), out_shape=ja...]
where the time goes in v4:
time: 25.7 us; the launch traced here: 25.5 us
  Pallas kernels  24.6 us (96%)
  local copies, waits for them, and re-layouts  0.97 us (4%)
    pallas_call x1, Pallas kernels, local(): pl.pallas_call(functools.partial(kernel, shares, far_share), out_shape=ja...  24.6 us
    unnamed x1, local copies, waits for them, and re-layouts  0.97 us

profile of v4, /device:TPU:1, one launch (start us, length us, event | category | flops | bytes accessed | tf_op | source)
XLA Modules:
  0.0 25.5 jit_solution(3040470332438589444)
XLA Ops:
  0.0 24.6 %shard_map.91 = f32[16,128,128]{2,1,0:T(8,128)S(1)} custom-call(f32[16,128,128]{2,1,0:T(8,128)} %x_hbm.1, bf16[32,128]{1,0:T(8,128)(2,1)} %constant.16.clone.refs_0_, bf16[256,256]{1,0:T(8,128)(2,1)} %constant.17.clone.refs_1_, bf16[128,256]{1,0:T(8,128)(2,1)} %constant.18.clone.refs_2_, bf16[136,256]{1,0:T(8,128)(2,1)} %constant.19.clone.refs_3_, ...), custom_call_target="tpu_custom_call" | custom-call | tf_op jit(solution)/shard_map/pallas_call | solution.py:482
  24.6 1.0 %copy.11 = f32[16,128,128]{2,1,0:T(8,128)} copy(f32[16,128,128]{2,1,0:T(8,128)S(1)} %shard_map.91) | data formatting | bytes 2097152

commit v5 on v4

--- a/solution.py
+++ b/solution.py
@@ -16,6 +16,7 @@
 ZETA = 1.149604398860241
 AXES = ("gz", "gx", "gy")
 BF16 = ml_dtypes.bfloat16
+X_RANKS = (2, 3, 4)
 
 
 def lifting_matrix(n):
@@ -71,7 +72,14 @@
     take[0:6], take[8:14] = r_before.T, r_after.T
     w_hi, w_lo = split(own.T)
     t_hi, t_lo = split(take)
-    ext = [np.concatenate([lv[1], lv[0][:w], lv[2][-w:]]) for lv, w in zip(per_level, (4, 8, 8))]
+    ext = []
+    for lv, w, slot, rows in zip(per_level, X_RANKS, (2, 4, 4), (136, 80, 48)):
+        m = np.zeros((rows, n))
+        own_rows = len(lv[1])
+        m[:own_rows] = lv[1]
+        m[own_rows : own_rows + w] = lv[0][:w]
+        m[own_rows + slot : own_rows + slot + w] = lv[2][-w:]
+        ext.append(m)
     g1_hi, g1_lo = split(ext[0])
     g2_hi, g2_lo = split(np.concatenate(ext[1:]))
     return dict(
@@ -84,6 +92,13 @@
         g2b=g2_lo,
         ra=np.concatenate([t_hi, t_hi, t_lo]),
     )
+
+
+def x_shares(n, total):
+    return [
+        (before[:8] @ np.linalg.pinv(before[:w], rcond=1e-9), after[-8:] @ np.linalg.pinv(after[-w:], rcond=1e-9))
+        for (before, _, after), w in zip(blocks(n, total), X_RANKS)
+    ]
 
 
 def level2_shares(n, total):
@@ -151,6 +166,9 @@
 
 
 SIDES = (1, -1)
+CHUNK = 4
+PLANES2 = (*range(8), 8, 9, 10, 12, 13, 14)
+PLANES3 = (*range(4), 8, 9, 10, 11, 12, 13, 14, 15, 16, 17, 18, 19)
 TARGETS = (
     [(a, b, 0) for a in (2, -2, 1, -1, 0) for b in SIDES]
     + [(a, 0, 0) for a in (2, -2, 1, -1)]
@@ -158,28 +176,33 @@
 )
 
 
-def kernel(shares, far_share, x_hbm, *refs):
+def kernel(edge_shares, shares, far_share, x_hbm, *refs):
     tables_hbm, out, x, tables_vmem, rest = refs[:8], refs[8], refs[9], refs[10:18], refs[18:]
     (
-        yc, q1, q2, q3, f2, f3, xc, ec,
+        yc, q1, qs, w, f2, f3, xc, ec,
         ys, yr, xs, xr, zs, zr, ts, tr, ps, pr, es, er, ds, dr, cs, cr,
         load_sem, send_sem, recv_sem,
     ) = rest
     nz, nx, ny = x.shape
     f32 = jnp.float32
 
-    loads = [pltpu.make_async_copy(x_hbm, x, load_sem.at[0])]
-    loads += [pltpu.make_async_copy(a, b, load_sem.at[k]) for k, (a, b) in enumerate(zip(tables_hbm, tables_vmem), 1)]
-    for load in loads[:2]:
+    x_loads = [
+        pltpu.make_async_copy(x_hbm.at[CHUNK * k : CHUNK * k + CHUNK], x.at[CHUNK * k : CHUNK * k + CHUNK], load_sem.at[k])
+        for k in range(nz // CHUNK)
+    ]
+    loads = [
+        pltpu.make_async_copy(a, b, load_sem.at[k]) for k, (a, b) in enumerate(zip(tables_hbm, tables_vmem), len(x_loads))
+    ]
+    for load in (*x_loads, loads[0]):
         load.start()
     sa, wa, wb, g1a, g1b, g2a, g2b, ra = tables_vmem
     barrier = pltpu.get_barrier_semaphore()
     for offsets in TARGETS:
         pl.semaphore_signal(barrier, inc=1, device_id=neighbour(offsets), device_id_type=pl.DeviceIdType.MESH)
-    for load in loads[2:]:
+    for load in loads[1:]:
         load.start()
 
-    copies = []
+    copies, p_copy, d_copy, c_copy, e_copy, t_copy, x_copy = [], {}, {}, {}, {}, {}, {}
 
     def send(source, target, offsets):
         k = len(copies)
@@ -194,24 +217,50 @@
     row = lax.broadcasted_iota(jnp.int32, (8, 128), 0)
     lane = lax.broadcasted_iota(jnp.int32, (8, 128), 1)
 
-    def pack_rows(one, two, side):
-        if side == 0:
-            return jnp.where(row < 4, one, pltpu.roll(two, 4, 0))
-        return jnp.where(row < 4, pltpu.roll(one, 4, 0), two)
-
-    def unpack_rows(packed, second, side):
-        v = packed if second == side else pltpu.roll(packed, 4, 0)
-        return jnp.where((row < 4) == (side == 0), v, 0.0)
+    def slots(parts, width, first):
+        total = None
+        for k, v in enumerate(parts):
+            amount = (k * width - first) % 8
+            v = pltpu.roll(v, amount, 0) if amount else v
+            total = v if total is None else jnp.where(row < k * width, total, v)
+        return total
+
+    columns = {}
+    for level, sides in enumerate(edge_shares):
+        for b, m in enumerate(sides):
+            for r in range(m.shape[1]):
+                column = jnp.zeros((8, 128), f32)
+                for k in range(8):
+                    if abs(m[k, r]) > 1e-12:
+                        column = jnp.where(row == k, float(m[k, r]), column)
+                columns[level, b, r] = column
+
+    def spread(level, b, v, first):
+        return sum(columns[level, b, r] * v[first + r : first + r + 1] for r in range(X_RANKS[level]))
+
+    def lane_of(v):
+        return lax.broadcasted_iota(jnp.int32, v.shape, 1)
 
     def pack2(one, two):
         two = jnp.zeros_like(one) if two is None else pltpu.roll(two, 1, 1)
-        return jnp.where(lane % 2 == 0, one, two)
+        return jnp.where(lane_of(one) % 2 == 0, one, two)
 
     def pack4(parts):
         total = parts[0]
         for k, part in enumerate(parts[1:], 1):
-            total = jnp.where(lane % 4 == (1 + k) % 4, pltpu.roll(part, k, 1), total)
+            total = jnp.where(lane_of(part) % 4 == (1 + k) % 4, pltpu.roll(part, k, 1), total)
         return total
+
+    def lift_level2(v):
+        c2, _, _ = lift_zero_extended(v, -4, nz + 3, True)
+        o, _, _ = lift_zero_extended({k // 2: w for k, w in c2.items()}, -3, 10)
+        return [o[k] for k in (*range(8), 8, 9, 10, -3, -2, -1)]
+
+    def lift_level3(v):
+        c2, _, _ = lift_zero_extended(v, -4, nz + 3, True)
+        c3, _, _ = lift_zero_extended({k // 2: w for k, w in c2.items()}, -6, 12, True)
+        o, _, _ = lift_zero_extended({k // 2: w for k, w in c3.items()}, -6, 10)
+        return [o[k] for k in (*range(4), 4, 5, 6, 7, -4, -3, -2, -1, 8, 9, -6, -5)]
 
     def shift(v, k):
         return pltpu.roll(v, 128 - k, 1) if k else v
@@ -228,16 +277,16 @@
 
     with jax.named_scope("load"):
         loads[0].wait()
-        loads[1].wait()
 
     with jax.named_scope("ymsg"):
-        hi, lo = halo_parts(x[...].reshape(nz * nx, ny))
-        first = dot(sa[...], hi, ((1,), (1,)))
-        second = dot(sa[0:16], lo, ((1,), (1,)))
-        message = first[0:16] + first[16:32] + second
-        for z in range(nz):
-            for c in range(2):
-                ys[c, z] = message[8 * c : 8 * c + 8, z * nx : (z + 1) * nx]
+        for k, load in enumerate(x_loads):
+            load.wait()
+            hi, lo = halo_parts(x[CHUNK * k : CHUNK * k + CHUNK].reshape(CHUNK * nx, ny))
+            first = dot(sa[...], hi, ((1,), (1,)))
+            message = first[0:16] + first[16:32] + dot(sa[0:16], lo, ((1,), (1,)))
+            for z in range(CHUNK):
+                for c in range(2):
+                    ys[c, CHUNK * k + z] = message[8 * c : 8 * c + 8, z * nx : (z + 1) * nx]
     with jax.named_scope("barw"):
         for tile in range(16):
             rows = slice(8 * tile, 8 * tile + 8)
@@ -252,11 +301,24 @@
         z_copies = [send(zs.at[a], zr.at[a], (s, 0, 0)) for a, s in enumerate(SIDES)]
 
     with jax.named_scope("ycent"):
-        for load in loads[2:]:
+        for load in loads[1:]:
             load.wait()
         for z in range(nz):
             hi, lo = halo_parts(x[z])
             yc[z] = dot(jnp.concatenate([hi, lo], axis=1), wa[...]) + dot(hi, wb[...])
+    with jax.named_scope("x2"):
+        for z in range(nz):
+            hi, lo = halo_parts(yc[z, :, deeper])
+            q = dot(g2a[...], jnp.concatenate([hi, lo], axis=0)) + dot(g2b[...], hi)
+            qs[z] = q
+
+    with jax.named_scope("z23"):
+        for tile in range(16):
+            rows = slice(8 * tile, 8 * tile + 8)
+            planes, lift = (PLANES2, lift_level2) if tile < 10 else (PLANES3, lift_level3)
+            for k, v in zip(planes, lift({k: qs[k, rows] for k in range(nz)})):
+                w[k, rows] = v
+
     with jax.named_scope("x1"):
         for z in range(nz):
             hi, lo = halo_parts(yc[z, :, level1])
@@ -274,13 +336,6 @@
                 for a in range(2):
                     for r in range(2):
                         ec[a, r] = pairs[a][r]
-        late = []
-    with jax.named_scope("x2"):
-        for z in range(nz):
-            hi, lo = halo_parts(yc[z, :, deeper])
-            q = dot(g2a[...], jnp.concatenate([hi, lo], axis=0)) + dot(g2b[...], hi)
-            q2[z] = q[0:80]
-            q3[z] = q[80:128]
 
     with jax.named_scope("ywait"):
         for copy in y_copies:
@@ -298,77 +353,69 @@
             (one, two), (three, four) = ((t[0:8, 0:nx], t[8:16, 0:nx]) for t in t1_pairs[a])
             second, fourth = jnp.where(row < 2, one, pltpu.roll(two, 2, 0)), jnp.where(row < 2, three, pltpu.roll(four, 2, 0))
             ts[a] = jnp.where(row < 4, second, pltpu.roll(fourth, 4, 0))
+        from2 = dict(zip(PLANES2, lift_level2({k: t2[k] for k in range(nz)})))
+        from3 = dict(zip(PLANES3, lift_level3({k: t2[k] for k in range(nz)})))
+        level2_rows = lax.broadcasted_iota(jnp.int32, (16, 128), 1) < 80
+
+    def halo_share(k):
+        if k in from2 and k in from3:
+            h = jnp.where(level2_rows, from2[k], from3[k])
+        elif k in from2:
+            h = jnp.where(level2_rows, from2[k], 0.0)
+        else:
+            h = jnp.where(level2_rows, 0.0, from3[k])
+        return expand(h, deeper)
+
+    with jax.named_scope("zplanes"):
+        for k in range(8, 20):
+            w[k] += halo_share(k)
+        edge1 = [[ec[a, r] + expand(t1_pairs[a][r][:, nx : nx + 8], level1) for r in range(2)] for a in range(2)]
+
+    with jax.named_scope("zpack"):
+        for a in range(2):
+            near = [w.at[8 + 4 * a + k] for k in range(4)]
+            ps[a, 0:64] = pack2(near[0][0:64], near[1][0:64])
+            odd = [pack2(near[k][80:112], pltpu.roll(near[k + 1][80:112], 1, 1)) for k in (0, 2)]
+            odd = [jnp.where(lane_of(v) % 4 == 3, v, near[2 * k][80:112]) for k, v in enumerate(odd)]
+            third = near[2][0:64]
+            ps[a, 64:128] = jnp.where(lane_of(third) % 2 == 0, third, jnp.concatenate(odd, axis=0))
+            far = [w.at[16 + 2 * a + k] for k in range(2)]
+            ds[a] = pack4([far[0][80:96], far[1][80:96], far[0][96:112], far[1][96:112]])
+            for b in range(2):
+                e = 2 * a + b
+                near3 = pack4([v[112:120] for v in near])
+                far3 = pack4([far[0][112:120], far[1][112:120], far[0][112:120], far[1][112:120]])
+                es[e, 0] = jnp.where(row < 4, slots(edge1[a], 2, 2 * b), pltpu.roll(near3, 4 - 4 * b, 0) if b == 0 else near3)
+                es[e, 1] = slots([pack2(near[0][64:72], near[1][64:72]), pack2(near[2][64:72], None)], 4, 4 * b)
+                cs[e] = slots([far3], 4, 4 * b)
         for a, s in enumerate(SIDES):
-            late.append(send(ts.at[a], tr.at[a], (s, 0, 0)))
-    with jax.named_scope("q23"):
-        for z in range(nz):
-            q = expand(t2[z], deeper)
-            q2[z] += q[0:80]
-            q3[z] += q[80:128]
-
-    with jax.named_scope("z23"):
-        for tile in (8, 9, 0, 1, 2, 3, 4, 5, 6, 7):
-            rows = slice(8 * tile, 8 * tile + 8)
-            c2, _, _ = lift_zero_extended({k: q2[k, rows] for k in range(nz)}, -4, nz + 3, True)
-            o, _, _ = lift_zero_extended({k // 2: w for k, w in c2.items()}, -3, 10)
-            if tile < 8:
-                for k in range(8):
-                    f2[k, rows] = o[k]
-            else:
-                for k in range(4):
-                    xs[tile - 8, 8 + k] = pack2(o[2 * k], o[2 * k + 1])
-            for a, (one, two, three) in enumerate(((8, 9, 10), (-3, -2, -1))):
-                for r, packed in enumerate((pack2(o[one], o[two]), pack2(o[three], None))):
-                    if tile < 8:
-                        ps[a, 64 * r + 8 * tile : 64 * r + 8 * tile + 8] = packed
-                    else:
-                        es[2 * a + tile - 8, 1 + r] = packed
-        kept = {}
-        for tile in range(6):
-            rows = slice(8 * tile, 8 * tile + 8)
-            c2, _, _ = lift_zero_extended({k: q3[k, rows] for k in range(nz)}, -4, nz + 3, True)
-            c3, _, _ = lift_zero_extended({k // 2: w for k, w in c2.items()}, -6, 12, True)
-            o, _, _ = lift_zero_extended({k // 2: w for k, w in c3.items()}, -6, 10)
-            if tile < 4:
-                for k in range(4):
-                    f3[k, rows] = o[k]
-            else:
-                xs[tile - 4, 12] = pack4([o[0], o[1], o[2], o[3]])
-            near = ((o[4], o[5], o[6], o[7]), (o[-4], o[-3], o[-2], o[-1]))
-            far = ((o[8], o[9]), (o[-6], o[-5]))
-            for a in range(2):
-                if tile < 4:
-                    for half in range(2):
-                        at = slice(64 + 32 * half + 8 * tile, 72 + 32 * half + 8 * tile)
-                        one, two = near[a][2 * half], near[a][2 * half + 1]
-                        odd = jnp.where(lane % 4 == 1, one, pltpu.roll(two, 2, 1))
-                        ps[a, at] = jnp.where(lane % 2 == 0, ps[a, at], odd)
-                    if tile < 2:
-                        kept[a, tile] = far[a]
-                    else:
-                        ds[a, 8 * tile - 16 : 8 * tile - 8] = pack4([*kept[a, tile - 2], *far[a]])
-                else:
-                    es[2 * a + tile - 4, 3] = pack4(near[a])
-                    cs[2 * a + tile - 4] = pack4([*far[a], *far[a]])
+            t_copy[a] = send(ts.at[a], tr.at[a], (s, 0, 0))
+            d_copy[a] = send(ds.at[a], dr.at[a], (2 * s, 0, 0))
+            for b, t in enumerate(SIDES):
+                e = 2 * a + b
+                c_copy[e] = send(cs.at[e], cr.at[e], (2 * s, t, 0))
+                e_copy[e] = send(es.at[e], er.at[e], (s, t, 0))
         for a, s in enumerate(SIDES):
-            late.append(send(ds.at[a], dr.at[a], (2 * s, 0, 0)))
-            late.append(send(ps.at[a], pr.at[a], (s, 0, 0)))
-            for b, t in enumerate(SIDES):
-                late.append(send(cs.at[2 * a + b], cr.at[2 * a + b], (2 * s, t, 0)))
+            p_copy[a] = send(ps.at[a], pr.at[a], (s, 0, 0))
 
     with jax.named_scope("xs"):
         full = [xc[k] + expand(t1[k][:, nx : nx + 8], level1) for k in range(nz)]
-        for k in range(nz // 2):
+        for k in range(nz // 4):
             for b in range(2):
-                xs[b, k] = pack_rows(full[2 * k], full[2 * k + 1], b)
-        for a in range(2):
-            full = [ec[a, r] + expand(t1_pairs[a][r][:, nx : nx + 8], level1) for r in range(2)]
-            for b in range(2):
-                es[2 * a + b, 0] = pack_rows(full[0], full[1], b)
+                xs[b, k] = slots(full[4 * k : 4 * k + 4], 2, 2 * b)
+        pairs2, thirds = [], []
+        for k in range(0, 8, 2):
+            one, two = w[k] + halo_share(k), w[k + 1] + halo_share(k + 1)
+            f2[k], f2[k + 1] = one[0:64], two[0:64]
+            pairs2.append(pack2(one[64:72], two[64:72]))
+            if k < 4:
+                f3[k], f3[k + 1] = one[80:112], two[80:112]
+                thirds += [one[112:120], two[112:120]]
         for b, t in enumerate(SIDES):
-            late.append(send(xs.at[b], xr.at[b], (0, t, 0)))
-            for a, s in enumerate(SIDES):
-                late.append(send(es.at[2 * a + b], er.at[2 * a + b], (s, t, 0)))
+            for k in range(2):
+                xs[b, 4 + k] = slots(pairs2[2 * k : 2 * k + 2], 4, 4 * b)
+            xs[b, 6] = slots([pack4(thirds)], 4, 4 * b)
+            x_copy[b] = send(xs.at[b], xr.at[b], (0, t, 0))
 
     with jax.named_scope("own1"):
         for k in range(nz):
@@ -384,10 +431,6 @@
                 hi, lo = halo_parts(y)
                 zr[a, r] = dot(g1a[0:nx], jnp.concatenate([hi, lo], axis=0)) + dot(g1b[0:nx], hi)
 
-    with jax.named_scope("wait2"):
-        for copy in late:
-            copy.wait_recv()
-
     def take_far(a, rows, v, first):
         one, two = shift(v, first), shift(v, first + 1)
         if a == 0:
@@ -398,29 +441,47 @@
             f3[2, rows] += one
             f3[3, rows] += two
 
-    with jax.named_scope("edges"):
+    ends = ((0, 0, 0), (nx - 8, nx // 2 - 8, nx // 4 - 8))
+    with jax.named_scope("wait_t"):
         for a in range(2):
+            t_copy[a].wait_recv()
             for r in range(2):
                 quad = pltpu.roll(tr[a], 4, 0) if r else tr[a]
                 quad = [jnp.where(row < 2, pltpu.roll(quad, 6, 0) if c else quad, 0.0) for c in range(2)]
                 zr[a, r] += expand(jnp.concatenate(quad, axis=0), level1)
-            for b, (r1, r2, r3) in enumerate(((0, 0, 0), (nx - 8, nx // 2 - 8, nx // 4 - 8))):
+
+    with jax.named_scope("wait_x"):
+        for b, (r1, r2, r3) in enumerate(ends):
+            x_copy[b].wait_recv()
+            for k in range(16):
+                out[k, r1 : r1 + 8] += spread(0, b, xr[b, k // 4], 2 * (k % 4))
+            for k in range(4):
+                pair = spread(1, b, xr[b, 4 + k // 2], 4 * (k % 2))
+                for q in range(2):
+                    f2[2 * k + q, r2 : r2 + 8] += shift(pair, q)
+            quad = spread(2, b, xr[b, 6], 0)
+            for k in range(4):
+                f3[k, r3 : r3 + 8] += shift(quad, k)
+
+    with jax.named_scope("wait_z"):
+        for group in (d_copy, c_copy, e_copy, p_copy):
+            for copy in group.values():
+                copy.wait_recv()
+    with jax.named_scope("edges"):
+        for a in range(2):
+            for half in range(2):
+                take_far(a, slice(16 * half, 16 * half + 16), dr[a], 2 * half)
+                for q in range(2):
+                    f3[2 * half + q] += shift(pr[a, 64 + 32 * half : 96 + 32 * half], 2 * q)
+            for b, (r1, r2, r3) in enumerate(ends):
                 e = 2 * a + b
                 for r in range(2):
-                    zr[a, r, r1 : r1 + 8] += unpack_rows(er[e, 0], r, b)
-                    pr[a, 64 * r + r2 : 64 * r + r2 + 8] += er[e, 1 + r]
+                    zr[a, r, r1 : r1 + 8] += spread(0, b, er[e, 0], 2 * r)
+                    pr[a, 64 * r + r2 : 64 * r + r2 + 8] += spread(1, b, er[e, 1], 4 * r)
+                quad = spread(2, b, er[e, 0], 4)
                 for j in range(4):
-                    f3[j, r3 : r3 + 8] += shift(er[e, 3], j)
-                take_far(a, slice(r3, r3 + 8), cr[e], 0)
-
-    with jax.named_scope("xfaces"):
-        for b, (r1, r2, r3) in enumerate(((0, 0, 0), (nx - 8, nx // 2 - 8, nx // 4 - 8))):
-            for k in range(16):
-                out[k, r1 : r1 + 8] += unpack_rows(xr[b, k // 2], k % 2, b)
-            for k in range(8):
-                f2[k, r2 : r2 + 8] += shift(xr[b, 8 + k // 2], k % 2)
-            for k in range(4):
-                f3[k, r3 : r3 + 8] += shift(xr[b, 12], k)
+                    f3[j, r3 : r3 + 8] += shift(quad, j)
+                take_far(a, slice(r3, r3 + 8), spread(2, b, cr[e], 0), 0)
 
     with jax.named_scope("zfaces"):
         for tile in range(16):
@@ -451,11 +512,6 @@
         for a in range(2):
             first, second = pr[a, 0:64], pr[a, 64:128]
             parts.append((first, shift(first, 1), second))
-            for half in range(2):
-                for q in range(2):
-                    f3[2 * half + q] += shift(pr[a, 64 + 32 * half : 96 + 32 * half], 2 * q)
-            for half in range(2):
-                take_far(a, slice(16 * half, 16 * half + 16), dr[a], 2 * half)
         for k in range(8):
             total = f2[k]
             for a in range(2):
@@ -473,32 +529,32 @@
             copy.wait_send()
 
 
-def local(turbulence, consts, shares, far_share):
+def local(turbulence, consts, edge_shares, shares, far_share):
     nz, nx, ny = turbulence.shape
     f32 = jnp.float32
     vmem = lambda *shape: pltpu.VMEM(shape, f32)
     pair = lambda *shape: [vmem(*shape), vmem(*shape)]
     count = 20
     return pl.pallas_call(
-        functools.partial(kernel, shares, far_share),
+        functools.partial(kernel, edge_shares, shares, far_share),
         out_shape=jax.ShapeDtypeStruct(turbulence.shape, f32),
         in_specs=[pl.BlockSpec(memory_space=pltpu.HBM)] * (1 + len(consts)),
         out_specs=pl.BlockSpec(memory_space=pltpu.VMEM),
         scratch_shapes=[
             vmem(nz, nx, ny),
             *[pltpu.VMEM(c.shape, c.dtype) for c in consts],
-            vmem(nz, nx, 2 * ny), vmem(nz, 136, ny), vmem(nz, 80, ny), vmem(nz, 48, ny),
+            vmem(nz, nx, 2 * ny), vmem(nz, 136, ny), vmem(nz, 128, ny), vmem(20, 128, ny),
             vmem(8, 64, ny), vmem(4, 32, ny),
             vmem(nz, 8, ny), vmem(2, 2, 8, ny),
             *pair(2, nz, 8, nx),
-            *pair(2, 13, 8, ny),
+            *pair(2, 7, 8, ny),
             *pair(2, 2, nx, ny),
             *pair(2, 8, nx),
             *pair(2, 128, ny),
-            *pair(4, 4, 8, ny),
+            *pair(4, 2, 8, ny),
             *pair(2, 16, ny),
             *pair(4, 8, ny),
-            pltpu.SemaphoreType.DMA((1 + len(consts),)),
+            pltpu.SemaphoreType.DMA((nz // CHUNK + len(consts),)),
             pltpu.SemaphoreType.DMA((count,)),
             pltpu.SemaphoreType.DMA((count,)),
         ],
@@ -511,8 +567,9 @@
         nz, n, _ = turbulence.shape
         t = tables(n, n * lax.axis_size("gx"))
         names = ("sa", "wa", "wb", "g1a", "g1b", "g2a", "g2b", "ra")
-        along_z = nz, nz * lax.axis_size("gz")
-        return local(turbulence, [jnp.asarray(t[k]) for k in names], level2_shares(*along_z), level3_shares(*along_z))
+        along_x, along_z = (n, n * lax.axis_size("gx")), (nz, nz * lax.axis_size("gz"))
+        consts = [jnp.asarray(t[k]) for k in names]
+        return local(turbulence, consts, x_shares(*along_x), level2_shares(*along_z), level3_shares(*along_z))
 
     spec = P(*AXES)
     return jax.shard_map(run, mesh=mesh, in_specs=(spec,), out_specs=spec, check_vma=False)

time: 25.7 us -> 25 us (0.973)
  Pallas kernels: 24.6 us -> 23.9 us
    pallas_call x1, Pallas kernels: 24.6 us -> 23.9 us  [local(): pl.pallas_call(functools.partial(kernel, edge_shares, shares, far_share),...]
where the time goes in v5:
time: 25 us; the launch traced here: 24.9 us
  Pallas kernels  23.9 us (96%)
  local copies, waits for them, and re-layouts  0.97 us (4%)
    pallas_call x1, Pallas kernels, local(): pl.pallas_call(functools.partial(kernel, edge_shares, shares, far_share),...  23.9 us
    unnamed x1, local copies, waits for them, and re-layouts  0.97 us

profile of v5, /device:TPU:1, one launch (start us, length us, event | category | flops | bytes accessed | tf_op | source)
XLA Modules:
  0.0 24.9 jit_solution(474164822100755349)
XLA Ops:
  0.0 23.9 %shard_map.91 = f32[16,128,128]{2,1,0:T(8,128)S(1)} custom-call(f32[16,128,128]{2,1,0:T(8,128)} %x_hbm.1, bf16[32,128]{1,0:T(8,128)(2,1)} %constant.16.clone.refs_0_, bf16[256,256]{1,0:T(8,128)(2,1)} %constant.17.clone.refs_1_, bf16[128,256]{1,0:T(8,128)(2,1)} %constant.18.clone.refs_2_, bf16[136,256]{1,0:T(8,128)(2,1)} %constant.19.clone.refs_3_, ...), custom_call_target="tpu_custom_call" | custom-call | tf_op jit(solution)/shard_map/pallas_call | solution.py:538
  23.9 1.0 %copy.11 = f32[16,128,128]{2,1,0:T(8,128)} copy(f32[16,128,128]{2,1,0:T(8,128)S(1)} %shard_map.91) | data formatting | bytes 2097152

commit v6 on v5

--- a/solution.py
+++ b/solution.py
@@ -170,8 +170,9 @@
 PLANES2 = (*range(8), 8, 9, 10, 12, 13, 14)
 PLANES3 = (*range(4), 8, 9, 10, 11, 12, 13, 14, 15, 16, 17, 18, 19)
 TARGETS = (
-    [(a, b, 0) for a in (2, -2, 1, -1, 0) for b in SIDES]
-    + [(a, 0, 0) for a in (2, -2, 1, -1)]
+    [(a, b, 0) for a in SIDES for b in SIDES]
+    + [(0, b, 0) for b in SIDES]
+    + [(a, 0, 0) for a in SIDES]
     + [(0, 0, c) for c in SIDES]
 )
 
@@ -193,7 +194,7 @@
     loads = [
         pltpu.make_async_copy(a, b, load_sem.at[k]) for k, (a, b) in enumerate(zip(tables_hbm, tables_vmem), len(x_loads))
     ]
-    for load in (*x_loads, loads[0]):
+    for load in (loads[0], *x_loads):
         load.start()
     sa, wa, wb, g1a, g1b, g2a, g2b, ra = tables_vmem
     barrier = pltpu.get_barrier_semaphore()
@@ -346,13 +347,7 @@
         hi, lo = halo_parts(h)
         both = jnp.concatenate([hi, lo], axis=1)
         rhs = ((1,), (1,))
-        t1 = (dot(both, g1a[...], rhs) + dot(hi, g1b[...], rhs)).reshape(nz, 16, 136)
         t2 = (dot(both, g2a[...], rhs) + dot(hi, g2b[...], rhs)).reshape(nz, 16, 128)
-        t1, t1_pairs = lift_level1({k: t1[k] for k in range(nz)})
-        for a in range(2):
-            (one, two), (three, four) = ((t[0:8, 0:nx], t[8:16, 0:nx]) for t in t1_pairs[a])
-            second, fourth = jnp.where(row < 2, one, pltpu.roll(two, 2, 0)), jnp.where(row < 2, three, pltpu.roll(four, 2, 0))
-            ts[a] = jnp.where(row < 4, second, pltpu.roll(fourth, 4, 0))
         from2 = dict(zip(PLANES2, lift_level2({k: t2[k] for k in range(nz)})))
         from3 = dict(zip(PLANES3, lift_level3({k: t2[k] for k in range(nz)})))
         level2_rows = lax.broadcasted_iota(jnp.int32, (16, 128), 1) < 80
@@ -369,7 +364,6 @@
     with jax.named_scope("zplanes"):
         for k in range(8, 20):
             w[k] += halo_share(k)
-        edge1 = [[ec[a, r] + expand(t1_pairs[a][r][:, nx : nx + 8], level1) for r in range(2)] for a in range(2)]
 
     with jax.named_scope("zpack"):
         for a in range(2):
@@ -381,22 +375,30 @@
             ps[a, 64:128] = jnp.where(lane_of(third) % 2 == 0, third, jnp.concatenate(odd, axis=0))
             far = [w.at[16 + 2 * a + k] for k in range(2)]
             ds[a] = pack4([far[0][80:96], far[1][80:96], far[0][96:112], far[1][96:112]])
+        for a, s in enumerate(SIDES):
+            p_copy[a] = send(ps.at[a], pr.at[a], (s, 0, 0))
+
+    with jax.named_scope("halo1"):
+        t1 = (dot(both, g1a[...], rhs) + dot(hi, g1b[...], rhs)).reshape(nz, 16, 136)
+        t1, t1_pairs = lift_level1({k: t1[k] for k in range(nz)})
+        for a in range(2):
+            (one, two), (three, four) = ((t[0:8, 0:nx], t[8:16, 0:nx]) for t in t1_pairs[a])
+            second, fourth = jnp.where(row < 2, one, pltpu.roll(two, 2, 0)), jnp.where(row < 2, three, pltpu.roll(four, 2, 0))
+            ts[a] = jnp.where(row < 4, second, pltpu.roll(fourth, 4, 0))
+        edge1 = [[ec[a, r] + expand(t1_pairs[a][r][:, nx : nx + 8], level1) for r in range(2)] for a in range(2)]
+        for a, s in enumerate(SIDES):
+            near, far = [w.at[8 + 4 * a + k] for k in range(4)], [w.at[16 + 2 * a + k] for k in range(2)]
+            near3 = pack4([v[112:120] for v in near])
+            far3 = pack4([far[0][112:120], far[1][112:120], far[0][112:120], far[1][112:120]])
             for b in range(2):
                 e = 2 * a + b
-                near3 = pack4([v[112:120] for v in near])
-                far3 = pack4([far[0][112:120], far[1][112:120], far[0][112:120], far[1][112:120]])
-                es[e, 0] = jnp.where(row < 4, slots(edge1[a], 2, 2 * b), pltpu.roll(near3, 4 - 4 * b, 0) if b == 0 else near3)
+                es[e, 0] = jnp.where(row < 4, slots(edge1[a], 2, 2 * b), pltpu.roll(near3, 4, 0) if b == 0 else near3)
                 es[e, 1] = slots([pack2(near[0][64:72], near[1][64:72]), pack2(near[2][64:72], None)], 4, 4 * b)
                 cs[e] = slots([far3], 4, 4 * b)
         for a, s in enumerate(SIDES):
             t_copy[a] = send(ts.at[a], tr.at[a], (s, 0, 0))
-            d_copy[a] = send(ds.at[a], dr.at[a], (2 * s, 0, 0))
             for b, t in enumerate(SIDES):
-                e = 2 * a + b
-                c_copy[e] = send(cs.at[e], cr.at[e], (2 * s, t, 0))
-                e_copy[e] = send(es.at[e], er.at[e], (s, t, 0))
-        for a, s in enumerate(SIDES):
-            p_copy[a] = send(ps.at[a], pr.at[a], (s, 0, 0))
+                e_copy[2 * a + b] = send(es.at[2 * a + b], er.at[2 * a + b], (s, t, 0))
 
     with jax.named_scope("xs"):
         full = [xc[k] + expand(t1[k][:, nx : nx + 8], level1) for k in range(nz)]
@@ -417,13 +419,20 @@
             xs[b, 6] = slots([pack4(thirds)], 4, 4 * b)
             x_copy[b] = send(xs.at[b], xr.at[b], (0, t, 0))
 
+    with jax.named_scope("zwait"):
+        for copy in z_copies:
+            copy.wait_recv()
+        for a, s in enumerate(SIDES):
+            d_copy[a] = send(ds.at[a], dr.at[a], (2 * s, 0, 0))
+        for a, s in enumerate(SIDES):
+            for b, t in enumerate(SIDES):
+                c_copy[2 * a + b] = send(cs.at[2 * a + b], cr.at[2 * a + b], (2 * s, t, 0))
+
     with jax.named_scope("own1"):
         for k in range(nz):
             out[k] += expand(t1[k][:, 0:nx], level1)
 
     with jax.named_scope("zraw"):
-        for copy in z_copies:
-            copy.wait_recv()
         for a in range(2):
             for r in range(2):
                 hi, lo = halo_parts(zr[a, r])

time: 25 us -> 24.6 us (0.984)
  Pallas kernels: 23.9 us -> 23.4 us
    pallas_call x1, Pallas kernels: 23.9 us -> 23.4 us  [local(): pl.pallas_call(functools.partial(kernel, edge_shares, shares, far_share),...]
where the time goes in v6:
time: 24.6 us; the launch traced here: 24.4 us
  Pallas kernels  23.4 us (95%)
  local copies, waits for them, and re-layouts  0.97 us (4%)
    pallas_call x1, Pallas kernels, local(): pl.pallas_call(functools.partial(kernel, edge_shares, shares, far_share),...  23.4 us
    unnamed x1, local copies, waits for them, and re-layouts  0.97 us

profile of v6, /device:TPU:1, one launch (start us, length us, event | category | flops | bytes accessed | tf_op | source)
XLA Modules:
  0.0 24.4 jit_solution(988917668970891102)
XLA Ops:
  0.0 23.4 %shard_map.91 = f32[16,128,128]{2,1,0:T(8,128)S(1)} custom-call(f32[16,128,128]{2,1,0:T(8,128)} %x_hbm.1, bf16[32,128]{1,0:T(8,128)(2,1)} %constant.16.clone.refs_0_, bf16[256,256]{1,0:T(8,128)(2,1)} %constant.17.clone.refs_1_, bf16[128,256]{1,0:T(8,128)(2,1)} %constant.18.clone.refs_2_, bf16[136,256]{1,0:T(8,128)(2,1)} %constant.19.clone.refs_3_, ...), custom_call_target="tpu_custom_call" | custom-call | tf_op jit(solution)/shard_map/pallas_call | solution.py:547
  23.4 1.0 %copy.11 = f32[16,128,128]{2,1,0:T(8,128)} copy(f32[16,128,128]{2,1,0:T(8,128)S(1)} %shard_map.91) | data formatting | bytes 2097152

commit v7 on v6

--- a/solution.py
+++ b/solution.py
@@ -169,12 +169,7 @@
 CHUNK = 4
 PLANES2 = (*range(8), 8, 9, 10, 12, 13, 14)
 PLANES3 = (*range(4), 8, 9, 10, 11, 12, 13, 14, 15, 16, 17, 18, 19)
-TARGETS = (
-    [(a, b, 0) for a in SIDES for b in SIDES]
-    + [(0, b, 0) for b in SIDES]
-    + [(a, 0, 0) for a in SIDES]
-    + [(0, 0, c) for c in SIDES]
-)
+TARGETS = [(0, b, 0) for b in SIDES] + [(a, 0, 0) for a in SIDES] + [(0, 0, c) for c in SIDES]
 
 
 def kernel(edge_shares, shares, far_share, x_hbm, *refs):
@@ -182,7 +177,7 @@
     (
         yc, q1, qs, w, f2, f3, xc, ec,
         ys, yr, xs, xr, zs, zr, ts, tr, ps, pr, es, er, ds, dr, cs, cr,
-        load_sem, send_sem, recv_sem,
+        load_sem, send_sem, recv_sem, hello_sem,
     ) = rest
     nz, nx, ny = x.shape
     f32 = jnp.float32
@@ -301,6 +296,14 @@
         y_copies = [send(ys.at[k], yr.at[k], (0, 0, c)) for k, c in enumerate(SIDES)]
         z_copies = [send(zs.at[a], zr.at[a], (s, 0, 0)) for a, s in enumerate(SIDES)]
 
+    def hello(first, directions):
+        for k, offsets in enumerate(directions):
+            pl.semaphore_signal(
+                hello_sem.at[first + k], inc=1, device_id=neighbour(offsets), device_id_type=pl.DeviceIdType.MESH
+            )
+
+    hello(0, [(a, 0, 0) for a in SIDES])
+
     with jax.named_scope("ycent"):
         for load in loads[1:]:
             load.wait()
@@ -320,6 +323,9 @@
             for k, v in zip(planes, lift({k: qs[k, rows] for k in range(nz)})):
                 w[k, rows] = v
 
+    for k in range(2):
+        pl.semaphore_wait(hello_sem.at[k], 1)
+    hello(2, [(0, b, 0) for b in SIDES])
     with jax.named_scope("x1"):
         for z in range(nz):
             hi, lo = halo_parts(yc[z, :, level1])
@@ -376,6 +382,8 @@
             far = [w.at[16 + 2 * a + k] for k in range(2)]
             ds[a] = pack4([far[0][80:96], far[1][80:96], far[0][96:112], far[1][96:112]])
         for a, s in enumerate(SIDES):
+            d_copy[a] = send(ds.at[a], dr.at[a], (2 * s, 0, 0))
+        for a, s in enumerate(SIDES):
             p_copy[a] = send(ps.at[a], pr.at[a], (s, 0, 0))
 
     with jax.named_scope("halo1"):
@@ -395,6 +403,11 @@
                 es[e, 0] = jnp.where(row < 4, slots(edge1[a], 2, 2 * b), pltpu.roll(near3, 4, 0) if b == 0 else near3)
                 es[e, 1] = slots([pack2(near[0][64:72], near[1][64:72]), pack2(near[2][64:72], None)], 4, 4 * b)
                 cs[e] = slots([far3], 4, 4 * b)
+        for k in (2, 3):
+            pl.semaphore_wait(hello_sem.at[k], 1)
+        for a, s in enumerate(SIDES):
+            for b, t in enumerate(SIDES):
+                c_copy[2 * a + b] = send(cs.at[2 * a + b], cr.at[2 * a + b], (2 * s, t, 0))
         for a, s in enumerate(SIDES):
             t_copy[a] = send(ts.at[a], tr.at[a], (s, 0, 0))
             for b, t in enumerate(SIDES):
@@ -422,11 +435,6 @@
     with jax.named_scope("zwait"):
         for copy in z_copies:
             copy.wait_recv()
-        for a, s in enumerate(SIDES):
-            d_copy[a] = send(ds.at[a], dr.at[a], (2 * s, 0, 0))
-        for a, s in enumerate(SIDES):
-            for b, t in enumerate(SIDES):
-                c_copy[2 * a + b] = send(cs.at[2 * a + b], cr.at[2 * a + b], (2 * s, t, 0))
 
     with jax.named_scope("own1"):
         for k in range(nz):
@@ -566,6 +574,7 @@
             pltpu.SemaphoreType.DMA((nz // CHUNK + len(consts),)),
             pltpu.SemaphoreType.DMA((count,)),
             pltpu.SemaphoreType.DMA((count,)),
+            pltpu.SemaphoreType.REGULAR((4,)),
         ],
         compiler_params=pltpu.CompilerParams(collective_id=0, has_side_effects=True, vmem_limit_bytes=48 << 20),
     )(*[pltpu.with_memory_space_constraint(a, pltpu.HBM) for a in (turbulence, *consts)])

time: 24.6 us -> 24.3 us (0.988)
  Pallas kernels: 23.4 us -> 23.1 us
    pallas_call x1, Pallas kernels: 23.4 us -> 23.1 us  [local(): pl.pallas_call(functools.partial(kernel, edge_shares, shares, far_share),...]
where the time goes in v7:
time: 24.3 us; the launch traced here: 24 us
  Pallas kernels  23.1 us (95%)
  local copies, waits for them, and re-layouts  0.97 us (4%)
    pallas_call x1, Pallas kernels, local(): pl.pallas_call(functools.partial(kernel, edge_shares, shares, far_share),...  23.1 us
    unnamed x1, local copies, waits for them, and re-layouts  0.97 us

profile of v7, /device:TPU:1, one launch (start us, length us, event | category | flops | bytes accessed | tf_op | source)
XLA Modules:
  0.0 24.0 jit_solution(862300980021047593)
XLA Ops:
  0.0 23.1 %shard_map.91 = f32[16,128,128]{2,1,0:T(8,128)S(1)} custom-call(f32[16,128,128]{2,1,0:T(8,128)} %x_hbm.1, bf16[32,128]{1,0:T(8,128)(2,1)} %constant.16.clone.refs_0_, bf16[256,256]{1,0:T(8,128)(2,1)} %constant.17.clone.refs_1_, bf16[128,256]{1,0:T(8,128)(2,1)} %constant.18.clone.refs_2_, bf16[136,256]{1,0:T(8,128)(2,1)} %constant.19.clone.refs_3_, ...), custom_call_target="tpu_custom_call" | custom-call | tf_op jit(solution)/shard_map/pallas_call | solution.py:555
  23.1 1.0 %copy.11 = f32[16,128,128]{2,1,0:T(8,128)} copy(f32[16,128,128]{2,1,0:T(8,128)S(1)} %shard_map.91) | data formatting | bytes 2097152

commit v8 on v7

--- a/solution.py
+++ b/solution.py
@@ -166,7 +166,7 @@
 
 
 SIDES = (1, -1)
-CHUNK = 4
+CHUNK = 2
 PLANES2 = (*range(8), 8, 9, 10, 12, 13, 14)
 PLANES3 = (*range(4), 8, 9, 10, 11, 12, 13, 14, 15, 16, 17, 18, 19)
 TARGETS = [(0, b, 0) for b in SIDES] + [(a, 0, 0) for a in SIDES] + [(0, 0, c) for c in SIDES]

time: 24.3 us -> 25 us (1.029)
  Pallas kernels: 23.1 us -> 23.8 us
    pallas_call x1, Pallas kernels: 23.1 us -> 23.8 us  [local(): pl.pallas_call(functools.partial(kernel, edge_shares, shares, far_share),...]
where the time goes in v8:
time: 25 us; the launch traced here: 24.7 us
  Pallas kernels  23.8 us (95%)
  local copies, waits for them, and re-layouts  0.97 us (4%)
    pallas_call x1, Pallas kernels, local(): pl.pallas_call(functools.partial(kernel, edge_shares, shares, far_share),...  23.8 us
    unnamed x1, local copies, waits for them, and re-layouts  0.97 us

profile of v8, /device:TPU:1, one launch (start us, length us, event | category | flops | bytes accessed | tf_op | source)
XLA Modules:
  0.0 24.7 jit_solution(4573742752519080022)
XLA Ops:
  0.0 23.8 %shard_map.91 = f32[16,128,128]{2,1,0:T(8,128)S(1)} custom-call(f32[16,128,128]{2,1,0:T(8,128)} %x_hbm.1, bf16[32,128]{1,0:T(8,128)(2,1)} %constant.16.clone.refs_0_, bf16[256,256]{1,0:T(8,128)(2,1)} %constant.17.clone.refs_1_, bf16[128,256]{1,0:T(8,128)(2,1)} %constant.18.clone.refs_2_, bf16[136,256]{1,0:T(8,128)(2,1)} %constant.19.clone.refs_3_, ...), custom_call_target="tpu_custom_call" | custom-call | tf_op jit(solution)/shard_map/pallas_call | solution.py:555
  23.8 1.0 %copy.11 = f32[16,128,128]{2,1,0:T(8,128)} copy(f32[16,128,128]{2,1,0:T(8,128)S(1)} %shard_map.91) | data formatting | bytes 2097152
